TPU v7x, 32 devices: a whole 2x2x4 slice. The times are simulated.
32 devices in a mesh: groups: 2 (over y), rows: 4 (over x, core), cols: 4 (over z).
Axes of the slice: x: 2, y: 2, z: 4, core: 2. Of those that a mesh axis runs over, the one named last changes fastest.
Arguments:
- object_field: float32 [4, 512, 1024], P('groups', 'cols', 'rows'), parts along dimension 0, may hold values from -6 to 6
- probe: float32 [8, 2, 512, 512], P('groups', None, 'cols'), parts along dimension 0, may hold values from -3 to 3
- amplitudes: float32 [48, 512, 512], P(('groups', 'rows'), 'cols'), parts along dimension 0, may hold values from 0.5 to 3.5
- strip_counts: int32 [8], P(('groups', 'rows')), parts along dimension 0, may hold values from 1 to 6, 12 in all
- row_offsets: int32 [48], P(('groups', 'rows')), parts along dimension 0, may hold values from 0 to 255
- col_offsets: int32 [48], P(('groups', 'rows')), parts along dimension 0, may hold values from 0 to 127
Outputs:
- object_grad: float32 [4, 512, 1024], P('groups', 'cols', 'rows'), parts along dimension 0
- probe_grad: float32 [8, 2, 512, 512], P('groups', None, 'cols'), parts along dimension 0
There are 2 independent parts, one for each index of `groups`. A program takes and returns all parts, laid end to end along the dimension named above; each array names one. Nothing has to cross between parts.
Inputs may be any that keep to these rules, and one draw needn't show every extreme that they name: `strip_counts`: the counts sum to 12, and the largest is exactly 6.
All inputs are finite; a program needn't handle non-finite values. No bound on the sum of `strip_counts` on one device may be relied on, other than what follows from the above.
Results may differ from a plain program's by a relative error of at most 0.012.
The roundings to bfloat16 on the way count: a program that leaves them out, or rounds other values in their place, can miss the bound.
Values may be sent and summed in bfloat16 or wider, within the bound.
A program may use at most 64 MiB of HBM per device.

v0:
```python
import jax
import jax.numpy as jnp
from jax import lax
from jax.sharding import PartitionSpec as P

POS_AVG = 3
POS_MAX = 6


def shifted(block, axis, distance):
    devices = range(lax.axis_size(axis))
    route = [(i - distance, i) for i in devices if i - distance in devices]
    return lax.ppermute(block, axis, route)


def dft_tables(length):
    indices = jnp.arange(length, dtype=jnp.int32)
    product = indices[:, None] * indices[None, :] % length
    angles = product.astype(jnp.float32) * jnp.float32(2.0 * 3.141592653589793 / length)
    scaling = jnp.float32(1.0 / length**0.5)
    cosine_table = (jnp.cos(angles) * scaling).astype(jnp.bfloat16)
    sine_table = (jnp.sin(angles) * scaling).astype(jnp.bfloat16)
    return (cosine_table, sine_table)


def leading(values, matrix):
    return jnp.einsum("mca,asu->mscu", values, matrix, preferred_element_type=jnp.float32)


def second(values, matrix):
    return jnp.einsum("mscu,scv->muv", values, matrix, preferred_element_type=jnp.float32)


def third(values, matrix):
    return jnp.einsum("muv,vsb->msub", values, matrix, preferred_element_type=jnp.float32)


def fourth(values, matrix):
    return jnp.einsum("msub,sua->mba", values, matrix, preferred_element_type=jnp.float32)


def vacuum_where(block, outside):
    fill_real = jnp.where(outside, jnp.float32(1.0), block[0])
    fill_imag = jnp.where(outside, jnp.float32(0.0), block[1])
    return jnp.stack([fill_real, fill_imag])


def spectral_pass(patch_cells, probe, measured, cosine_table, sine_table, block_count):
    mode_count = probe.shape[0]
    block_cols = patch_cells.shape[1]
    length = patch_cells.shape[2]
    block_freq = length // block_count
    probe_real = probe[:, 0]
    probe_imag = probe[:, 1]
    patch_real = patch_cells[0]
    patch_imag = patch_cells[1]
    wave_real = (probe_real * patch_real - probe_imag * patch_imag).astype(jnp.bfloat16)
    wave_imag = (probe_real * patch_imag + probe_imag * patch_real).astype(jnp.bfloat16)
    cos_lead = cosine_table.reshape(length, block_count, block_freq)
    sin_lead = sine_table.reshape(length, block_count, block_freq)
    first_real = leading(wave_real, cos_lead) + leading(wave_imag, sin_lead)
    first_imag = leading(wave_imag, cos_lead) - leading(wave_real, sin_lead)
    outgoing = jnp.stack([first_real, first_imag], axis=1).astype(jnp.bfloat16)
    outgoing = outgoing.reshape(mode_count, 2, block_count, block_cols * block_freq)
    arrived = lax.all_to_all(outgoing, "cols", split_axis=2, concat_axis=2, tiled=True)
    arrived = arrived.reshape(mode_count, 2, block_count, block_cols, block_freq)
    cos_rows = cosine_table.reshape(block_count, block_cols, length)
    sin_rows = sine_table.reshape(block_count, block_cols, length)
    field_real = second(arrived[:, 0], cos_rows) + second(arrived[:, 1], sin_rows)
    field_imag = second(arrived[:, 1], cos_rows) - second(arrived[:, 0], sin_rows)
    intensity = jnp.sum(field_real * field_real + field_imag * field_imag, axis=0)
    modulus = jnp.sqrt(jnp.maximum(intensity, 0.25))
    factor = 1.0 - measured / modulus
    back_real = (field_real * factor).astype(jnp.bfloat16)
    back_imag = (field_imag * factor).astype(jnp.bfloat16)
    cos_back = cosine_table.reshape(length, block_count, block_cols)
    sin_back = sine_table.reshape(length, block_count, block_cols)
    inner_real = third(back_real, cos_back) - third(back_imag, sin_back)
    inner_imag = third(back_imag, cos_back) + third(back_real, sin_back)
    returning = jnp.stack([inner_real, inner_imag], axis=1).astype(jnp.bfloat16)
    returning = returning.reshape(mode_count, 2, block_count, block_freq * block_cols)
    landed = lax.all_to_all(returning, "cols", split_axis=2, concat_axis=2, tiled=True)
    landed = landed.reshape(mode_count, 2, block_count, block_freq, block_cols)
    cos_freq = cosine_table.reshape(block_count, block_freq, length)
    sin_freq = sine_table.reshape(block_count, block_freq, length)
    grad_real = fourth(landed[:, 0], cos_freq) - fourth(landed[:, 1], sin_freq)
    grad_imag = fourth(landed[:, 1], cos_freq) + fourth(landed[:, 0], sin_freq)
    object_real = jnp.sum(probe_real * grad_real + probe_imag * grad_imag, axis=0)
    object_imag = jnp.sum(probe_real * grad_imag - probe_imag * grad_real, axis=0)
    probe_real_term = patch_real * grad_real + patch_imag * grad_imag
    probe_imag_term = patch_real * grad_imag - patch_imag * grad_real
    return (
        jnp.stack([object_real, object_imag]),
        jnp.stack([probe_real_term, probe_imag_term], axis=1),
    )


def run_positions(
    window,
    probe,
    frames,
    first_rows,
    first_cols,
    slot_total,
    used_count,
    cosine_table,
    sine_table,
    block_count,
):
    block_cols = probe.shape[2]
    length = probe.shape[3]

    def visit_slot(slot_index, state_pair):
        window_grad, probe_sum = state_pair
        first_row = first_rows[slot_index]
        first_col = first_cols[slot_index]
        patch_cells = lax.dynamic_slice(window, (0, first_col, first_row), (2, block_cols, length))
        measured = lax.dynamic_index_in_dim(frames, slot_index, 0, keepdims=False)
        object_term, probe_term = spectral_pass(
            patch_cells, probe, measured, cosine_table, sine_table, block_count
        )
        active = (slot_index < used_count).astype(jnp.float32)
        current = lax.dynamic_slice(window_grad, (0, first_col, first_row), (2, block_cols, length))
        window_grad = lax.dynamic_update_slice(
            window_grad, current + active * object_term, (0, first_col, first_row)
        )
        return (window_grad, probe_sum + active * probe_term)

    initial = (jnp.zeros(window.shape, jnp.float32), jnp.zeros(probe.shape, jnp.float32))
    return lax.fori_loop(0, slot_total, visit_slot, initial)


def on_device(object_field, probe, amplitudes, strip_counts, row_offsets, col_offsets):
    block_cols = object_field.shape[1]
    strip_rows = object_field.shape[2]
    length = probe.shape[3]
    block_count = lax.axis_size("cols")
    strip_total = lax.axis_size("rows")
    cosine_table, sine_table = dft_tables(length)
    beside = shifted(object_field, "cols", -1)
    beside = vacuum_where(beside, lax.axis_index("cols") == block_count - 1)
    paired = jnp.concatenate([object_field, beside], axis=1)
    counts_all, rows_all, cols_all = (
        lax.all_gather(strip_counts, "rows", axis=0, tiled=True),
        lax.all_gather(row_offsets, "rows", axis=0, tiled=True),
        lax.all_gather(col_offsets, "rows", axis=0, tiled=True),
    )
    totals = jnp.cumsum(counts_all)
    starts = totals - counts_all
    position_block = (lax.axis_index("rows") + strip_total // 2) % strip_total
    my_positions = position_block * POS_AVG + jnp.arange(POS_AVG, dtype=jnp.int32)
    strip_of = jnp.sum((totals[None, :] <= my_positions[:, None]).astype(jnp.int32), axis=1)
    wanted = strip_of * POS_MAX + my_positions - jnp.take(starts, strip_of)
    first_rows = strip_of * strip_rows + jnp.take(rows_all, wanted)
    first_cols = jnp.take(cols_all, wanted)
    empty_frames = jnp.zeros((POS_AVG,) + amplitudes.shape[1:], jnp.float32)
    received = lax.all_gather(amplitudes, "rows", axis=0, tiled=True)
    inside = (wanted >= 0) & (wanted < received.shape[0])
    picked = jnp.take(received, jnp.clip(wanted, 0, received.shape[0] - 1), axis=0)
    frames = jnp.where(inside[:, None, None], picked, empty_frames)
    column_all = lax.all_gather(paired, "rows", axis=2, tiled=True)
    all_rows = column_all.shape[2]
    vacuum_tail = vacuum_where(jnp.zeros((2, column_all.shape[1], length), jnp.float32), True)
    window = jnp.concatenate([column_all, vacuum_tail], axis=2)
    window_grad, probe_sum = run_positions(
        window,
        probe,
        frames,
        first_rows,
        first_cols,
        POS_AVG,
        POS_AVG,
        cosine_table,
        sine_table,
        block_count,
    )
    folded = window_grad[:, :, :all_rows]
    summed = lax.psum_scatter(folded, "rows", scatter_dimension=2, tiled=True)
    upper_half = shifted(summed[:, block_cols:], "cols", 1)
    object_grad = summed[:, :block_cols] + upper_half
    probe_grad = lax.psum(probe_sum, "rows")
    return (object_grad, probe_grad)


def solution(mesh):
    placed = (
        P("groups", "cols", "rows"),
        P("groups", None, "cols", None),
        P(("groups", "rows"), "cols", None),
        P(("groups", "rows")),
        P(("groups", "rows")),
        P(("groups", "rows")),
    )
    return jax.shard_map(
        on_device,
        mesh=mesh,
        in_specs=placed,
        out_specs=(P("groups", "cols", "rows"), P("groups", None, "cols", None)),
        check_vma=False,
    )
```

profile of v0, /device:TPU:9, one launch (start us, length us, event | category | flops | bytes accessed | tf_op | source)
XLA Modules:
  0.0 549.2 jit_solution(6323390557205095305)
XLA Ops:
  7.2 1.9 collective-permute-start
  9.2 7.3 %collective-permute-done = f32[2,128,256]{2,1,0:T(8,128)S(1)} collective-permute-done((f32[2,128,256]{2,1,0:T(8,128)}, f32[2,128,256]{2,1,0:T(8,128)S(1)}, u32[]{:S(2)}, u32[]{:S(2)}) %collective-permute-start) | collective-permute-done | bytes 262176 | tf_op jit(solution)/shard_map/ppermute | solution.py:13
  16.5 1.8 maximum_maximum_fusion
  22.3 5.1 all-reduce.3
  29.8 1.9 copy.90
  31.7 10.8 %all-gather.3.cloned.1.call-done = f32[2,256,1024]{2,1,0:T(8,128)} async-done(((f32[2,256,256]{2,1,0:T(8,128)}), f32[2,256,1024]{2,1,0:T(8,128)}) %all-gather.3.cloned.1.call-update) | async-done | bytes 2097168 | tf_op jit(solution)/shard_map/all_gather | solution.py:161
  42.7 3.6 pad_maximum_fusion.2
  46.3 44.4 %all-gather.5.cloned.1.call-done = f32[24,128,512]{2,1,0:T(8,128)} async-done(((f32[6,128,512]{2,1,0:T(8,128)}), f32[24,128,512]{2,1,0:T(8,128)}) %all-gather.5.cloned.1.call-update) | async-done | bytes 6291472 | tf_op jit(solution)/shard_map/all_gather | solution.py:157
  90.6 3.4 gather_fusion.1
  95.1 2.0 broadcast_in_dim.51
  97.1 350.3 %while.17 = (s32[]{:T(128)}, f32[2,256,1536]{2,1,0:T(8,128)}, f32[4,2,128,512]{3,2,0,1:T(8,128)}, s32[3]{0:T(128)S(1)}, s32[3]{0:T(128)S(1)}, /*index=5*/f32[4,2...) while((s32[]{:T(128)}, f32[2,256,1536]{2,1,0:T(8,128)}, ...), condition=%wide.region_6.8_spmd.clone.clone, body=%wide.region_2.7_spmd.clone.clone.sunk | while | flops 4321443840 | bytes 125829640 | solution.py:130
  97.1 4.0 multiply_convert_fusion.7
  101.1 4.0 multiply_convert_fusion.6
  112.4 1.5 fusion.157
  115.5 1.7 fusion.158
  118.4 3.2 pad_maximum_fusion.5
  121.6 4.6 all-to-all-start
  126.6 21.9 %all-to-all-done = bf16[4,2,4,16384]{3,1,0,2:T(2,128)(2,1)S(1)} async-done(((bf16[4,2,4,16384]{3,1,0,2:T(2,128)(2,1)}), bf16[4,2,4,16384]{3,1,0,2:T(2,128)(2,1)S(1)}, u32[]{:S(2)}, u32[]{:S(2)}) %all-to-all-start) | async-done | bytes 1048608 | tf_op jit(solution)/shard_map/while/body/eval_jaxpr/all_to_all | solution.py:65
  148.5 1.6 reshape.363
  150.1 2.1 fusion.159
  160.9 3.2 pad_maximum_fusion.6
  164.1 6.5 %all-to-all-start.1 = ((bf16[4,2,4,16384]{3,1,0,2:T(2,128)(2,1)}), bf16[4,2,4,16384]{3,1,0,2:T(2,128)(2,1)S(1)}, u32[]{:S(2)}, u32[]{:S(2)}) async-start(bf16[4,2,4,16384]{3,1,0,2:T(2,128)(2,1)} %pad_maximum_fusion.6), calls=%async_computation.1 | async-start | bytes 2097152 | tf_op jit(solution)/shard_map/while/body/eval_jaxpr/all_to_all | solution.py:82
  170.6 21.4 %all-to-all-done.1 = bf16[4,2,4,16384]{3,1,0,2:T(2,128)(2,1)S(1)} async-done(((bf16[4,2,4,16384]{3,1,0,2:T(2,128)(2,1)}), bf16[4,2,4,16384]{3,1,0,2:T(2,128)(2,1)S(1)}, u32[]{:S(2)}, u32[]{:S(2)}) %all-to-all-start.1) | async-done | bytes 1048608 | tf_op jit(solution)/shard_map/while/body/eval_jaxpr/all_to_all | solution.py:82
  197.2 4.0 add_bitcast_fusion.2
  202.6 5.7 %dynamic_update_slice.10 = f32[2,256,1536]{2,1,0:T(8,128)} dynamic-update-slice(f32[2,256,1536]{2,1,0:T(8,128)} %get-tuple-element.451, f32[2,128,512]{2,1,0:T(8,128)S(1)} %maximum_add_fusion.4, s32[]{:T(128)} %constant.141.clone.1..sunk, s32[]{:T(128)S(6)} %select_n.252, s32[]{:T(128)S(6)} %select_n.253) | dynamic-update-slice | bytes 1048580 | tf_op jit(solution)/shard_map/while/body/eval_jaxpr/dynamic_update_slice | solution.py:124
  208.3 3.2 maximum_add_fusion.5
  211.5 4.0 multiply_convert_fusion.7
  215.5 4.0 multiply_convert_fusion.6
  226.7 1.5 fusion.157
  229.9 1.7 fusion.158
  232.8 3.2 pad_maximum_fusion.5
  236.0 7.3 %all-to-all-start = ((bf16[4,2,4,16384]{3,1,0,2:T(2,128)(2,1)}), bf16[4,2,4,16384]{3,1,0,2:T(2,128)(2,1)S(1)}, u32[]{:S(2)}, u32[]{:S(2)}) async-start(bf16[4,2,4,16384]{3,1,0,2:T(2,128)(2,1)} %pad_maximum_fusion.5), calls=%async_computation | async-start | bytes 2097152 | tf_op jit(solution)/shard_map/while/body/eval_jaxpr/all_to_all | solution.py:65
  243.7 20.4 %all-to-all-done = bf16[4,2,4,16384]{3,1,0,2:T(2,128)(2,1)S(1)} async-done(((bf16[4,2,4,16384]{3,1,0,2:T(2,128)(2,1)}), bf16[4,2,4,16384]{3,1,0,2:T(2,128)(2,1)S(1)}, u32[]{:S(2)}, u32[]{:S(2)}) %all-to-all-start) | async-done | bytes 1048608 | tf_op jit(solution)/shard_map/while/body/eval_jaxpr/all_to_all | solution.py:65
  264.1 1.6 reshape.363
  265.7 2.1 fusion.159
  276.5 3.2 pad_maximum_fusion.6
  279.8 7.9 %all-to-all-start.1 = ((bf16[4,2,4,16384]{3,1,0,2:T(2,128)(2,1)}), bf16[4,2,4,16384]{3,1,0,2:T(2,128)(2,1)S(1)}, u32[]{:S(2)}, u32[]{:S(2)}) async-start(bf16[4,2,4,16384]{3,1,0,2:T(2,128)(2,1)} %pad_maximum_fusion.6), calls=%async_computation.1 | async-start | bytes 2097152 | tf_op jit(solution)/shard_map/while/body/eval_jaxpr/all_to_all | solution.py:82
  287.7 21.3 %all-to-all-done.1 = bf16[4,2,4,16384]{3,1,0,2:T(2,128)(2,1)S(1)} async-done(((bf16[4,2,4,16384]{3,1,0,2:T(2,128)(2,1)}), bf16[4,2,4,16384]{3,1,0,2:T(2,128)(2,1)S(1)}, u32[]{:S(2)}, u32[]{:S(2)}) %all-to-all-start.1) | async-done | bytes 1048608 | tf_op jit(solution)/shard_map/while/body/eval_jaxpr/all_to_all | solution.py:82
  314.1 4.0 add_bitcast_fusion.2
  319.5 6.3 %dynamic_update_slice.10 = f32[2,256,1536]{2,1,0:T(8,128)} dynamic-update-slice(f32[2,256,1536]{2,1,0:T(8,128)} %get-tuple-element.451, f32[2,128,512]{2,1,0:T(8,128)S(1)} %maximum_add_fusion.4, s32[]{:T(128)} %constant.141.clone.1..sunk, s32[]{:T(128)S(6)} %select_n.252, s32[]{:T(128)S(6)} %select_n.253) | dynamic-update-slice | bytes 1048580 | tf_op jit(solution)/shard_map/while/body/eval_jaxpr/dynamic_update_slice | solution.py:124
  325.8 3.9 maximum_add_fusion.5
  329.7 4.0 multiply_convert_fusion.7
  333.7 4.0 multiply_convert_fusion.6
  348.1 1.7 fusion.158
  351.0 3.2 pad_maximum_fusion.5
  354.2 7.4 %all-to-all-start = ((bf16[4,2,4,16384]{3,1,0,2:T(2,128)(2,1)}), bf16[4,2,4,16384]{3,1,0,2:T(2,128)(2,1)S(1)}, u32[]{:S(2)}, u32[]{:S(2)}) async-start(bf16[4,2,4,16384]{3,1,0,2:T(2,128)(2,1)} %pad_maximum_fusion.5), calls=%async_computation | async-start | bytes 2097152 | tf_op jit(solution)/shard_map/while/body/eval_jaxpr/all_to_all | solution.py:65
  362.0 21.1 %all-to-all-done = bf16[4,2,4,16384]{3,1,0,2:T(2,128)(2,1)S(1)} async-done(((bf16[4,2,4,16384]{3,1,0,2:T(2,128)(2,1)}), bf16[4,2,4,16384]{3,1,0,2:T(2,128)(2,1)S(1)}, u32[]{:S(2)}, u32[]{:S(2)}) %all-to-all-start) | async-done | bytes 1048608 | tf_op jit(solution)/shard_map/while/body/eval_jaxpr/all_to_all | solution.py:65
  383.1 1.6 reshape.363
  384.7 2.1 fusion.159
  395.5 3.2 pad_maximum_fusion.6
  398.7 7.2 %all-to-all-start.1 = ((bf16[4,2,4,16384]{3,1,0,2:T(2,128)(2,1)}), bf16[4,2,4,16384]{3,1,0,2:T(2,128)(2,1)S(1)}, u32[]{:S(2)}, u32[]{:S(2)}) async-start(bf16[4,2,4,16384]{3,1,0,2:T(2,128)(2,1)} %pad_maximum_fusion.6), calls=%async_computation.1 | async-start | bytes 2097152 | tf_op jit(solution)/shard_map/while/body/eval_jaxpr/all_to_all | solution.py:82
  405.9 21.3 %all-to-all-done.1 = bf16[4,2,4,16384]{3,1,0,2:T(2,128)(2,1)S(1)} async-done(((bf16[4,2,4,16384]{3,1,0,2:T(2,128)(2,1)}), bf16[4,2,4,16384]{3,1,0,2:T(2,128)(2,1)S(1)}, u32[]{:S(2)}, u32[]{:S(2)}) %all-to-all-start.1) | async-done | bytes 1048608 | tf_op jit(solution)/shard_map/while/body/eval_jaxpr/all_to_all | solution.py:82
  432.4 4.0 add_bitcast_fusion.2
  437.8 5.7 %dynamic_update_slice.10 = f32[2,256,1536]{2,1,0:T(8,128)} dynamic-update-slice(f32[2,256,1536]{2,1,0:T(8,128)} %get-tuple-element.451, f32[2,128,512]{2,1,0:T(8,128)S(1)} %maximum_add_fusion.4, s32[]{:T(128)} %constant.141.clone.1..sunk, s32[]{:T(128)S(6)} %select_n.252, s32[]{:T(128)S(6)} %select_n.253) | dynamic-update-slice | bytes 1048580 | tf_op jit(solution)/shard_map/while/body/eval_jaxpr/dynamic_update_slice | solution.py:124
  443.5 3.9 maximum_add_fusion.5
  447.4 3.2 slice.77
  450.7 1.5 copy-done.7
  452.2 1.6 copy.91
  453.8 31.5 %reduce-scatter.2.cloned.1.call-done = f32[2,256,256]{2,1,0:T(8,128)} async-done(((f32[2,256,1024]{2,1,0:T(8,128)}), f32[2,256,256]{2,1,0:T(8,128)}) %reduce-scatter.2.cloned.1.call-update) | async-done | bytes 524304 | tf_op jit(solution)/shard_map/reduce_scatter | solution.py:178
  486.3 3.1 collective-permute-start.1
  489.4 5.9 %collective-permute-done.1 = f32[2,128,256]{2,1,0:T(8,128)S(1)} collective-permute-done((f32[2,128,256]{2,1,0:T(8,128)S(1)}, f32[2,128,256]{2,1,0:T(8,128)S(1)}, u32[]{:S(2)}, u32[]{:S(2)}) %collective-permute-start.1) | collective-permute-done | bytes 262176 | tf_op jit(solution)/shard_map/ppermute | solution.py:13
  495.3 1.7 slice_add_fusion
  497.0 42.5 %all-reduce.6.cloned.1.call-done = f32[4,2,128,512]{3,2,1,0:T(8,128)} async-done(((f32[4,2,128,512]{3,2,1,0:T(8,128)}), f32[4,2,128,512]{3,2,1,0:T(8,128)}) %all-reduce.6.cloned.1.call-update) | async-done | bytes 2097168 | tf_op jit(solution)/shard_map/psum | solution.py:181
  539.6 3.1 copy.173
  (193 shorter events, 73.9 us)
Async XLA Ops:
  7.2 12.7 %copy-start.11 = (u32[32]{0:T(128)S(1)}, u32[32]{0:T(128)}, u32[]{:S(2)}) copy-start(u32[32]{0:T(128)} %constant.166) | copy-start | bytes 388
  7.2 13.9 %copy-start.9 = (s32[6]{0:T(128)S(1)}, s32[6]{0:T(128)}, u32[]{:S(2)}) copy-start(s32[6]{0:T(128)} %param.15) | copy-start | bytes 76
  7.2 14.2 %copy-start.10 = (s32[6]{0:T(128)S(1)}, s32[6]{0:T(128)}, u32[]{:S(2)}) copy-start(s32[6]{0:T(128)} %param.14) | copy-start | bytes 76
  7.2 35.3 %all-gather.3.cloned.1.call-start = ((), (), s32[]{:S(2)}) async-start(), calls=%async_computation.3 | async-start | bytes 2621440 | tf_op jit(solution)/shard_map/all_gather | solution.py:161
  7.2 9.3 %collective-permute-start = (f32[2,128,256]{2,1,0:T(8,128)}, f32[2,128,256]{2,1,0:T(8,128)S(1)}, u32[]{:S(2)}, u32[]{:S(2)}) collective-permute-start(f32[2,128,256]{2,1,0:T(8,128)} %param.10), channel_id=1, source_target_pairs={{1,0},{2,1},{3,2},{5,4},{6,5},{7,6},{9,8},{10,9},{11,10},{13,12},{... | collective-permute-start | bytes 786440 | tf_op jit(solution)/shard_map/ppermute | solution.py:13
  18.4 72.3 %all-gather.5.cloned.1.call-start = ((), (), s32[]{:S(2)}) async-start(), calls=%async_computation.4 | async-start | bytes 7864320 | tf_op jit(solution)/shard_map/all_gather | solution.py:157
  19.1 466.2 %reduce-scatter.2.cloned.1.call-start = ((), (), s32[]{:S(2)}) async-start(), calls=%async_computation.5 | async-start | bytes 2621440 | tf_op jit(solution)/shard_map/reduce_scatter | solution.py:178
  29.8 12.7 %copy-start.8 = (f32[2]{0:T(128)S(1)}, f32[2]{0:T(128)}, u32[]{:S(2)}) copy-start(f32[2]{0:T(128)} %constant.152.clone.1) | copy-start | bytes 28
  97.1 14.7 %copy-start = (f32[4,2,128,512]{3,2,0,1:T(8,128)}, f32[4,2,128,512]{3,2,0,1:T(8,128)S(1)}, u32[]{:S(2)}) copy-start(f32[4,2,128,512]{3,2,0,1:T(8,128)S(1)} %get-tuple-element.468) | copy-start | bytes 6291460 | tf_op jit(solution)/shard_map/while
  111.5 0.9 copy-start.5
  111.9 2.0 copy-start.2
  113.8 1.7 copy-start.3
  121.6 26.9 %all-to-all-start = ((bf16[4,2,4,16384]{3,1,0,2:T(2,128)(2,1)}), bf16[4,2,4,16384]{3,1,0,2:T(2,128)(2,1)S(1)}, u32[]{:S(2)}, u32[]{:S(2)}) async-start(bf16[4,2,4,16384]{3,1,0,2:T(2,128)(2,1)} %pad_maximum_fusion.5), calls=%async_computation | async-start | bytes 2097152 | tf_op jit(solution)/shard_map/while/body/eval_jaxpr/all_to_all | solution.py:65
  164.1 27.9 %all-to-all-start.1 = ((bf16[4,2,4,16384]{3,1,0,2:T(2,128)(2,1)}), bf16[4,2,4,16384]{3,1,0,2:T(2,128)(2,1)S(1)}, u32[]{:S(2)}, u32[]{:S(2)}) async-start(bf16[4,2,4,16384]{3,1,0,2:T(2,128)(2,1)} %pad_maximum_fusion.6), calls=%async_computation.1 | async-start | bytes 2097152 | tf_op jit(solution)/shard_map/while/body/eval_jaxpr/all_to_all | solution.py:82
  196.2 1.0 copy-start.6
  201.2 7.1 %copy-start.4 = (f32[4,1,128,512]{3,2,0,1:T(8,128)S(1)}, f32[4,1,128,512]{3,2,0,1:T(8,128)}, u32[]{:S(2)}) copy-start(f32[4,1,128,512]{3,2,0,1:T(8,128)} %get-tuple-element.436) | copy-start | bytes 3145732 | tf_op jit(solution)/shard_map/while
  208.3 3.2 copy-start.1
  211.5 14.7 %copy-start = (f32[4,2,128,512]{3,2,0,1:T(8,128)}, f32[4,2,128,512]{3,2,0,1:T(8,128)S(1)}, u32[]{:S(2)}) copy-start(f32[4,2,128,512]{3,2,0,1:T(8,128)S(1)} %get-tuple-element.468) | copy-start | bytes 6291460 | tf_op jit(solution)/shard_map/while
  225.9 0.9 copy-start.5
  226.2 2.0 copy-start.2
  228.2 1.7 copy-start.3
  236.0 28.1 %all-to-all-start = ((bf16[4,2,4,16384]{3,1,0,2:T(2,128)(2,1)}), bf16[4,2,4,16384]{3,1,0,2:T(2,128)(2,1)S(1)}, u32[]{:S(2)}, u32[]{:S(2)}) async-start(bf16[4,2,4,16384]{3,1,0,2:T(2,128)(2,1)} %pad_maximum_fusion.5), calls=%async_computation | async-start | bytes 2097152 | tf_op jit(solution)/shard_map/while/body/eval_jaxpr/all_to_all | solution.py:65
  279.8 29.2 %all-to-all-start.1 = ((bf16[4,2,4,16384]{3,1,0,2:T(2,128)(2,1)}), bf16[4,2,4,16384]{3,1,0,2:T(2,128)(2,1)S(1)}, u32[]{:S(2)}, u32[]{:S(2)}) async-start(bf16[4,2,4,16384]{3,1,0,2:T(2,128)(2,1)} %pad_maximum_fusion.6), calls=%async_computation.1 | async-start | bytes 2097152 | tf_op jit(solution)/shard_map/while/body/eval_jaxpr/all_to_all | solution.py:82
  313.2 1.0 copy-start.6
  318.1 7.7 %copy-start.4 = (f32[4,1,128,512]{3,2,0,1:T(8,128)S(1)}, f32[4,1,128,512]{3,2,0,1:T(8,128)}, u32[]{:S(2)}) copy-start(f32[4,1,128,512]{3,2,0,1:T(8,128)} %get-tuple-element.436) | copy-start | bytes 3145732 | tf_op jit(solution)/shard_map/while
  325.8 3.9 copy-start.1
  329.7 14.7 %copy-start = (f32[4,2,128,512]{3,2,0,1:T(8,128)}, f32[4,2,128,512]{3,2,0,1:T(8,128)S(1)}, u32[]{:S(2)}) copy-start(f32[4,2,128,512]{3,2,0,1:T(8,128)S(1)} %get-tuple-element.468) | copy-start | bytes 6291460 | tf_op jit(solution)/shard_map/while
  344.0 0.9 copy-start.5
  344.4 2.0 copy-start.2
  346.4 1.7 copy-start.3
  354.2 28.9 %all-to-all-start = ((bf16[4,2,4,16384]{3,1,0,2:T(2,128)(2,1)}), bf16[4,2,4,16384]{3,1,0,2:T(2,128)(2,1)S(1)}, u32[]{:S(2)}, u32[]{:S(2)}) async-start(bf16[4,2,4,16384]{3,1,0,2:T(2,128)(2,1)} %pad_maximum_fusion.5), calls=%async_computation | async-start | bytes 2097152 | tf_op jit(solution)/shard_map/while/body/eval_jaxpr/all_to_all | solution.py:65
  398.7 28.5 %all-to-all-start.1 = ((bf16[4,2,4,16384]{3,1,0,2:T(2,128)(2,1)}), bf16[4,2,4,16384]{3,1,0,2:T(2,128)(2,1)S(1)}, u32[]{:S(2)}, u32[]{:S(2)}) async-start(bf16[4,2,4,16384]{3,1,0,2:T(2,128)(2,1)} %pad_maximum_fusion.6), calls=%async_computation.1 | async-start | bytes 2097152 | tf_op jit(solution)/shard_map/while/body/eval_jaxpr/all_to_all | solution.py:82
  431.4 1.0 copy-start.6
  436.4 7.1 %copy-start.4 = (f32[4,1,128,512]{3,2,0,1:T(8,128)S(1)}, f32[4,1,128,512]{3,2,0,1:T(8,128)}, u32[]{:S(2)}) copy-start(f32[4,1,128,512]{3,2,0,1:T(8,128)} %get-tuple-element.436) | copy-start | bytes 3145732 | tf_op jit(solution)/shard_map/while
  443.5 3.9 copy-start.1
  450.6 1.6 copy-start.7
  450.6 89.0 %all-reduce.6.cloned.1.call-start = ((), (), s32[]{:S(2)}) async-start(), calls=%async_computation.6 | async-start | bytes 4194304 | tf_op jit(solution)/shard_map/psum | solution.py:181
  486.3 9.1 %collective-permute-start.1 = (f32[2,128,256]{2,1,0:T(8,128)S(1)}, f32[2,128,256]{2,1,0:T(8,128)S(1)}, u32[]{:S(2)}, u32[]{:S(2)}) collective-permute-start(f32[2,128,256]{2,1,0:T(8,128)S(1)} %slice.111), channel_id=1, source_target_pairs={{0,1},{1,2},{2,3},{4,5},{5,6},{6,7},{8,9},{9,10},{10,11},{12,13},{... | collective-permute-start | bytes 786440 | tf_op jit(solution)/shard_map/ppermute | solution.py:13
Sparse Core Ops, SparseCore 0:
  18.5 23.9 all-gather.2
  44.1 46.5 all-gather.4
  450.7 34.5 reduce-scatter.1
  488.2 51.3 all-reduce.5
where the time goes:
time: 554 us; the launch traced here: 549 us
  waiting for transfers between devices  271 us (49%)
  local copies, waits for them, and re-layouts  89.6 us (16%)
  other arithmetic  71.1 us (13%)
  starting transfers between devices  46.1 us (8%)
  matrix products  39.2 us (7%)
  between operations  15.3 us (3%)
  loops' own time  12.4 us (2%)
    all_to_all x3, waiting for transfers between devices, spectral_pass(): lax.all_to_all(returning, 'cols', split_axis=2, concat_axis=2, tiled=True)  64 us
    all_to_all x3, waiting for transfers between devices, spectral_pass(): lax.all_to_all(outgoing, 'cols', split_axis=2, concat_axis=2, tiled=True)  63.3 us
    all_gather x1, waiting for transfers between devices, on_device(): received = lax.all_gather(amplitudes, 'rows', axis=0, tiled=True)  44.4 us
    psum x1, waiting for transfers between devices, on_device(): probe_grad = lax.psum(probe_sum, 'rows')  42.5 us
    reduce_scatter x1, waiting for transfers between devices, on_device(): summed = lax.psum_scatter(folded, 'rows', scatter_dimension=2, tiled=True)  31.5 us
    all_to_all x3, starting transfers between devices, spectral_pass(): lax.all_to_all(returning, 'cols', split_axis=2, concat_axis=2, tiled=True)  21.6 us
    all_to_all x3, starting transfers between devices, spectral_pass(): lax.all_to_all(outgoing, 'cols', split_axis=2, concat_axis=2, tiled=True)  19.3 us
    dynamic_update_slice x3, local copies, waits for them, and re-layouts, visit_slot(): lax.dynamic_update_slice(window_grad, current + active * object_term, (0,...  17.8 us
  transfers between devices with their start and end apart: 12, of which 12 were waited for; matrix products, arithmetic and copies ran while one was open for 3% of the time, Pallas kernels for 0%

commit v1 on v0

--- a/solution.py
+++ b/solution.py
@@ -1,6 +1,11 @@
+import functools
+
 import jax
 import jax.numpy as jnp
+import numpy as np
 from jax import lax
+from jax.experimental import pallas as pl
+from jax.experimental.pallas import tpu as pltpu
 from jax.sharding import PartitionSpec as P
 
 POS_AVG = 3
@@ -130,7 +135,7 @@
     return lax.fori_loop(0, slot_total, visit_slot, initial)
 
 
-def on_device(object_field, probe, amplitudes, strip_counts, row_offsets, col_offsets):
+def general_device(object_field, probe, amplitudes, strip_counts, row_offsets, col_offsets):
     block_cols = object_field.shape[1]
     strip_rows = object_field.shape[2]
     length = probe.shape[3]
@@ -182,7 +187,421 @@
     return (object_grad, probe_grad)
 
 
+def tables(length):
+    indices = np.arange(length)
+    angles = (indices[:, None] * indices[None, :] % length) * (2.0 * np.pi / length)
+    scaling = 1.0 / length**0.5
+    return jnp.asarray(np.cos(angles) * scaling, jnp.bfloat16), jnp.asarray(np.sin(angles) * scaling, jnp.bfloat16)
+
+
+ANY = pl.BlockSpec(memory_space=pl.ANY)
+WHOLE = pl.BlockSpec(memory_space=pltpu.VMEM)
+LIMIT = 56 * 1024 * 1024
+N = 4
+
+
+def greet(axes):
+    barrier = pltpu.get_barrier_semaphore()
+    for axis in axes:
+        me = lax.axis_index(axis)
+        for k in range(1, N):
+            pl.semaphore_signal(
+                barrier, inc=1, device_id={axis: lax.rem(me + k, N)}, device_id_type=pl.DeviceIdType.MESH
+            )
+    pl.semaphore_wait(barrier, (N - 1) * len(axes))
+
+
+def remote(src, dst, sems, slot, device):
+    return pltpu.make_async_remote_copy(
+        src_ref=src,
+        dst_ref=dst,
+        send_sem=sems.at[0, slot],
+        recv_sem=sems.at[1, slot],
+        device_id=device,
+        device_id_type=pl.DeviceIdType.MESH,
+    )
+
+
+class Gather:
+    def __init__(self, axis, src, out, sems, base, scatter=False):
+        self.me = lax.axis_index(axis)
+        self.axis, self.src, self.out, self.sems, self.base, self.scatter = axis, src, out, sems, base, scatter
+
+    def piece(self, index):
+        return self.src.at[index] if self.scatter else self.src
+
+    def start(self):
+        self.local = pltpu.make_async_copy(
+            self.piece(self.me), self.out.at[self.me], self.sems.at[0, self.base]
+        )
+        self.sent = []
+        for k in range(1, N):
+            to = lax.rem(self.me + k, N)
+            copy = remote(self.piece(to), self.out.at[self.me], self.sems, self.base + k, {self.axis: to})
+            copy.start()
+            self.sent.append(copy)
+        self.local.start()
+
+    def wait(self):
+        self.local.wait()
+        for k in range(1, N):
+            source = lax.rem(self.me + N - k, N)
+            remote(
+                self.piece(source), self.out.at[source], self.sems, self.base + k, {self.axis: source}
+            ).wait_recv()
+        for copy in self.sent:
+            copy.wait_send()
+
+
+def spread_inputs(meta, probe, cells, frames, meta_out, probe_out, cells_out, frames_out, sems):
+    row, col = lax.axis_index("rows"), lax.axis_index("cols")
+    sibling = row + 1 - 2 * lax.rem(row, 2)
+    across = lax.rem(row + 2, N)
+    greet(("rows", "cols"))
+    blocks = Gather("cols", cells, cells_out.at[row], sems, 0)
+    blocks.start()
+    small = Gather("rows", meta, meta_out, sems, 4)
+    small.start()
+    modes = Gather("cols", probe, probe_out, sems, 8)
+    modes.start()
+    local_frames = pltpu.make_async_copy(frames, frames_out.at[row], sems.at[0, 12])
+
+    @pl.when(row == col)
+    def _():
+        local_frames.start()
+
+    for k in range(1, N):
+
+        @pl.when(lax.rem(row + k, N) == col)
+        def _():
+            remote(frames, frames_out.at[row], sems, 12 + k, {"rows": lax.rem(row + k, N)}).start()
+
+    started = []
+    for k in range(N):
+        source = lax.rem(col + N - k, N)
+        mine = cells_out.at[row, source]
+        if k == 0:
+            blocks.local.wait()
+        else:
+            remote(cells, mine, sems, k, {"cols": source}).wait_recv()
+        for slot, to in ((16 + k, across), (20 + k, sibling)):
+            copy = remote(mine, mine, sems, slot, {"rows": to})
+            copy.start()
+            started.append(copy)
+    for k in range(N):
+        source = lax.rem(col + N - k, N)
+        landed = cells_out.at[across, source]
+        remote(landed, landed, sems, 16 + k, {"rows": across}).wait_recv()
+        copy = remote(landed, landed, sems, 24 + k, {"rows": sibling})
+        copy.start()
+        started.append(copy)
+    opposite = lax.rem(sibling + 2, N)
+    for k in range(N):
+        source = lax.rem(col + N - k, N)
+        near = cells_out.at[sibling, source]
+        remote(near, near, sems, 20 + k, {"rows": sibling}).wait_recv()
+        far = cells_out.at[opposite, source]
+        remote(far, far, sems, 24 + k, {"rows": sibling}).wait_recv()
+    for copy in started + blocks.sent:
+        copy.wait_send()
+    small.wait()
+    modes.wait()
+
+    @pl.when(row == col)
+    def _():
+        local_frames.wait()
+        for k in range(1, N):
+            source = lax.rem(row + N - k, N)
+            remote(frames, frames_out.at[source], sems, 12 + k, {"rows": source}).wait_recv()
+
+    for k in range(1, N):
+
+        @pl.when(lax.rem(row + k, N) == col)
+        def _():
+            remote(frames, frames_out.at[row], sems, 12 + k, {"rows": lax.rem(row + k, N)}).wait_send()
+
+
+def exchange_intensity(intensity, frames, parts_out, frames_out, sems):
+    row, col = lax.axis_index("rows"), lax.axis_index("cols")
+    greet(("rows", "cols"))
+    parts = Gather("rows", intensity, parts_out, sems, 0, scatter=True)
+    parts.start()
+
+    @pl.when(row == col)
+    def _():
+        local = pltpu.make_async_copy(frames.at[col], frames_out, sems.at[0, 4])
+        copies = []
+        for k in range(1, N):
+            to = lax.rem(col + k, N)
+            copies.append(remote(frames.at[to], frames_out, sems, 4 + k, {"cols": to}))
+            copies[-1].start()
+        local.start()
+        local.wait()
+        for copy in copies:
+            copy.wait_send()
+
+    for k in range(1, N):
+
+        @pl.when(lax.rem(row + k, N) == col)
+        def _():
+            remote(frames.at[col], frames_out, sems, 4 + k, {"cols": row}).wait_recv()
+
+    parts.wait()
+
+
+def gather_factors(factor, out, sems):
+    greet(("rows",))
+    job = Gather("rows", factor, out, sems, 0)
+    job.start()
+    job.wait()
+
+
+def scatter_gradients(probe_grad, cells_grad, probe_out, cells_out, sems):
+    greet(("rows", "cols"))
+    jobs = [
+        Gather("cols", probe_grad, probe_out, sems, 0, scatter=True),
+        Gather("rows", cells_grad, cells_out, sems, 4, scatter=True),
+    ]
+    for job in jobs:
+        job.start()
+    for job in jobs:
+        job.wait()
+
+
+def finish_gradients(cells_grad, probe_grad, cells_out, probe_out, sems):
+    greet(("rows", "cols"))
+    jobs = [
+        Gather("cols", cells_grad, cells_out, sems, 0, scatter=True),
+        Gather("rows", probe_grad, probe_out, sems, 4),
+    ]
+    for job in jobs:
+        job.start()
+    for job in jobs:
+        job.wait()
+
+
+def communicate(kernel, number, slots, outs, *args):
+    return pl.pallas_call(
+        kernel,
+        out_shape=[jax.ShapeDtypeStruct(shape, dtype) for shape, dtype in outs],
+        in_specs=[ANY] * len(args),
+        out_specs=[ANY] * len(outs),
+        scratch_shapes=[pltpu.SemaphoreType.DMA((2, slots))],
+        compiler_params=pltpu.CompilerParams(collective_id=number, has_side_effects=True),
+        name=kernel.__name__,
+    )(*args)
+
+
+def mul(left, right):
+    return jnp.dot(left, right, preferred_element_type=jnp.float32)
+
+
+def mul_t(left, right):
+    return lax.dot_general(left, right, (((1,), (1,)), ((), ())), preferred_element_type=jnp.float32)
+
+
+def forward(rows, cols, cells, probe, cosine, sine, patch_out, field_out, power_out, window):
+    p = pl.program_id(0)
+    strips, blocks, _, width, depth = cells.shape
+    length = cosine.shape[0]
+    all_rows, all_cols = strips * depth, blocks * width
+
+    @pl.when(p == 0)
+    def _():
+        for part, fill in ((0, 1.0), (1, 0.0)):
+            window[part, all_cols:, :] = jnp.full((width, window.shape[2]), fill, jnp.float32)
+            window[part, :all_cols, all_rows:] = jnp.full((all_cols, length), fill, jnp.float32)
+            for s in range(strips):
+                for b in range(blocks):
+                    window[part, pl.ds(b * width, width), pl.ds(s * depth, depth)] = cells[s, b, part].astype(
+                        jnp.float32
+                    )
+
+    first = rows[p]
+    rest = lax.rem(first, 128)
+    base = pl.multiple_of(first - rest, 128)
+    span = length + 128
+    patch = []
+    for part in range(2):
+        block = pltpu.roll(window[part, :, pl.ds(base, span)], lax.rem(span - rest, span), 1)[:, :length]
+        tall = window.shape[1]
+        patch.append(pltpu.roll(block, lax.rem(tall - cols[p], tall), 0)[:length])
+        patch_out[0, part] = patch[part].astype(jnp.bfloat16)
+    probe_real = probe[:, 0].reshape(length, length).astype(jnp.float32)
+    probe_imag = probe[:, 1].reshape(length, length).astype(jnp.float32)
+    wave_real = (probe_real * patch[0] - probe_imag * patch[1]).astype(jnp.bfloat16)
+    wave_imag = (probe_real * patch[1] + probe_imag * patch[0]).astype(jnp.bfloat16)
+    c, s = cosine[...], sine[...]
+    spread_real = (mul_t(c, wave_real) + mul_t(s, wave_imag)).astype(jnp.bfloat16)
+    spread_imag = (mul_t(c, wave_imag) - mul_t(s, wave_real)).astype(jnp.bfloat16)
+    field_real = mul(spread_real, c) + mul(spread_imag, s)
+    field_imag = mul(spread_imag, c) - mul(spread_real, s)
+    field_out[0, 0] = field_real
+    field_out[0, 1] = field_imag
+    power = field_real * field_real + field_imag * field_imag
+    power_out[:, 0] = power.reshape(N, length // N, length).astype(jnp.bfloat16)
+
+
+def backward(
+    rows, cols, factor, field, patch, probe, cosine, sine, probe_out, cells_out, window, total, padded
+):
+    p = pl.program_id(0)
+    strips, blocks, _, width, depth = cells_out.shape
+    length = cosine.shape[0]
+    span = length + 128
+
+    @pl.when(p == 0)
+    def _():
+        window[...] = jnp.zeros(window.shape, jnp.float32)
+        total[...] = jnp.zeros(total.shape, jnp.float32)
+        padded[...] = jnp.zeros(padded.shape, jnp.float32)
+
+    scale = factor[:, 0].reshape(length, length).astype(jnp.float32)
+    c, s = cosine[...], sine[...]
+    corrected_real = (field[0, 0] * scale).astype(jnp.bfloat16)
+    corrected_imag = (field[0, 1] * scale).astype(jnp.bfloat16)
+    inner_real = (mul_t(c, corrected_real) - mul_t(s, corrected_imag)).astype(jnp.bfloat16)
+    inner_imag = (mul_t(c, corrected_imag) + mul_t(s, corrected_real)).astype(jnp.bfloat16)
+    back_real = mul(inner_real, c) - mul(inner_imag, s)
+    back_imag = mul(inner_imag, c) + mul(inner_real, s)
+    patch_real = patch[0, 0].astype(jnp.float32)
+    patch_imag = patch[0, 1].astype(jnp.float32)
+    total[0] += patch_real * back_real + patch_imag * back_imag
+    total[1] += patch_real * back_imag - patch_imag * back_real
+    probe_real = probe[:, 0].reshape(length, length).astype(jnp.float32)
+    probe_imag = probe[:, 1].reshape(length, length).astype(jnp.float32)
+    first = rows[p]
+    rest = lax.rem(first, 128)
+    base = pl.multiple_of(first - rest, 128)
+    for part in range(2):
+        if part == 0:
+            term = probe_real * back_real + probe_imag * back_imag
+        else:
+            term = probe_real * back_imag - probe_imag * back_real
+        padded[:length, :length] = term
+        window[part, :, pl.ds(base, span)] += pltpu.roll(pltpu.roll(padded[...], cols[p], 0), rest, 1)
+
+    @pl.when(p == pl.num_programs(0) - 1)
+    def _():
+        for part in range(2):
+            for b in range(blocks):
+                probe_out[b, part] = total[part, pl.ds(b * width, width), :].astype(jnp.bfloat16)
+                for s in range(strips):
+                    cells_out[s, b, part] = window[part, pl.ds(b * width, width), pl.ds(s * depth, depth)].astype(
+                        jnp.bfloat16
+                    )
+
+
+def balanced_device(object_field, probe, amplitudes, strip_counts, row_offsets, col_offsets):
+    f32, bf16 = jnp.float32, jnp.bfloat16
+    width, depth = object_field.shape[1:]
+    length = probe.shape[3]
+    row, col = lax.axis_index("rows"), lax.axis_index("cols")
+    cosine, sine = tables(length)
+    meta = jnp.concatenate([strip_counts, row_offsets, col_offsets])
+    meta = jnp.pad(meta, (0, 128 - meta.shape[0]))[None, :]
+    meta = jnp.broadcast_to(meta, (8, 128))
+    mode = lax.dynamic_index_in_dim(probe, row, 0, keepdims=False).astype(bf16)
+    meta_all, mode_all, cells, frames_all = communicate(
+        spread_inputs,
+        1,
+        28,
+        [
+            ((N, 8, 128), jnp.int32),
+            ((N,) + mode.shape, bf16),
+            ((N, N) + object_field.shape, bf16),
+            ((N,) + amplitudes.shape, bf16),
+        ],
+        meta,
+        mode,
+        object_field.astype(bf16),
+        amplitudes.astype(bf16),
+    )
+    counts = meta_all[:, 0, 0]
+    totals = jnp.cumsum(counts)
+    starts = totals - counts
+    ids = jnp.arange(POS_AVG * N, dtype=jnp.int32)
+    strip_of = jnp.sum((totals[None, :] <= ids[:, None]).astype(jnp.int32), axis=1)
+    slot = strip_of * POS_MAX + ids - jnp.take(starts, strip_of)
+    rows_all = meta_all[:, 0, 1 : 1 + POS_MAX].reshape(-1)
+    cols_all = meta_all[:, 0, 1 + POS_MAX : 1 + 2 * POS_MAX].reshape(-1)
+    mine = lax.dynamic_slice(slot, (col * POS_AVG,), (POS_AVG,))
+    my_strip = lax.dynamic_slice(strip_of, (col * POS_AVG,), (POS_AVG,))
+    first_rows = my_strip * depth + jnp.take(rows_all, mine)
+    first_cols = jnp.take(cols_all, mine)
+    frames = jnp.take(frames_all.reshape((-1,) + amplitudes.shape[1:]), slot, axis=0)
+    frames = frames.reshape((N, POS_AVG) + amplitudes.shape[1:])
+
+    plane = (1, 2, length, length)
+    whole = lambda *shape: pl.BlockSpec(shape, lambda p, *_: (0,) * len(shape))
+    per_slot = pl.BlockSpec(plane, lambda p, *_: (p, 0, 0, 0))
+    quarters = pl.BlockSpec((N, 1, length // N, length), lambda p, *_: (0, p, 0, 0))
+    window = pltpu.VMEM((2, N * width + 128, N * depth + length), f32)
+    patch, field, power = pl.pallas_call(
+        forward,
+        grid_spec=pltpu.PrefetchScalarGridSpec(
+            num_scalar_prefetch=2,
+            grid=(POS_AVG,),
+            in_specs=[
+                whole(*cells.shape),
+                whole(*mode_all.shape),
+                whole(length, length),
+                whole(length, length),
+            ],
+            out_specs=[per_slot, per_slot, quarters],
+            scratch_shapes=[window],
+        ),
+        out_shape=[
+            jax.ShapeDtypeStruct((POS_AVG,) + plane[1:], bf16),
+            jax.ShapeDtypeStruct((POS_AVG,) + plane[1:], f32),
+            jax.ShapeDtypeStruct((N, POS_AVG, length // N, length), bf16),
+        ],
+        compiler_params=pltpu.CompilerParams(vmem_limit_bytes=LIMIT),
+        name="forward",
+    )(first_rows, first_cols, cells, mode_all, cosine, sine)
+    powers, measured = communicate(
+        exchange_intensity, 2, 8, [(power.shape, bf16), (power.shape[1:], bf16)], power, frames
+    )
+    intensity = jnp.sum(powers.astype(f32), axis=0)
+    factor = 1.0 - measured.astype(f32) * lax.rsqrt(jnp.maximum(intensity, 0.25))
+    (factors,) = communicate(gather_factors, 3, 4, [(power.shape, bf16)], factor.astype(bf16))
+    probe_part, cells_part = pl.pallas_call(
+        backward,
+        grid_spec=pltpu.PrefetchScalarGridSpec(
+            num_scalar_prefetch=2,
+            grid=(POS_AVG,),
+            in_specs=[
+                quarters,
+                per_slot,
+                per_slot,
+                whole(*mode_all.shape),
+                whole(length, length),
+                whole(length, length),
+            ],
+            out_specs=[whole(*mode_all.shape), whole(*cells.shape)],
+            scratch_shapes=[
+                window,
+                pltpu.VMEM((2, length, length), f32),
+                pltpu.VMEM((window.shape[1], length + 128), f32),
+            ],
+        ),
+        out_shape=[jax.ShapeDtypeStruct(mode_all.shape, bf16), jax.ShapeDtypeStruct(cells.shape, bf16)],
+        compiler_params=pltpu.CompilerParams(vmem_limit_bytes=LIMIT),
+        name="backward",
+    )(first_rows, first_cols, factors, field, patch, mode_all, cosine, sine)
+    probe_parts, cells_parts = communicate(
+        scatter_gradients, 4, 8, [(probe_part.shape, bf16), (cells_part.shape, bf16)], probe_part, cells_part
+    )
+    probe_sum = jnp.sum(probe_parts.astype(f32), axis=0).astype(bf16)
+    cells_sum = jnp.sum(cells_parts.astype(f32), axis=0).astype(bf16)
+    cells_last, probe_last = communicate(
+        finish_gradients, 5, 8, [(cells_sum.shape, bf16), ((N,) + probe_sum.shape, bf16)], cells_sum, probe_sum
+    )
+    return jnp.sum(cells_last.astype(f32), axis=0), probe_last.astype(f32)
+
+
 def solution(mesh):
+    on_device = balanced_device if mesh.shape["rows"] == N and mesh.shape["cols"] == N else general_device
     placed = (
         P("groups", "cols", "rows"),
         P("groups", None, "cols", None),

time: 554 us -> 200 us (0.36)
  waiting for transfers between devices: 271 us -> 0 us
  Pallas kernels: 0 us -> 167 us
  local copies, waits for them, and re-layouts: 89.6 us -> 9.12 us
  other arithmetic: 71.1 us -> 19.8 us
  starting transfers between devices: 46.1 us -> 0 us
  matrix products: 39.2 us -> 0 us
  between operations: 15.3 us -> 1.54 us
  loops' own time: 12.4 us -> 0 us
    pallas_call x0 -> x7, Pallas kernels: none -> 167 us  [the longest x5 127 us: communicate(): pl.pallas_call(kernel, out_shape=[jax.ShapeDtypeStruct(shape, dtype) for...]
    all_to_all x6 -> x0, waiting for transfers between devices: 127 us -> none  [the longest x3 64 us: spectral_pass(): lax.all_to_all(returning, 'cols', split_axis=2, concat_axis=2, tiled=True)]
    all_gather x2 -> x0, waiting for transfers between devices: 55.2 us -> none  [the longest x1 44.4 us: on_device(): received = lax.all_gather(amplitudes, 'rows', axis=0, tiled=True)]
    psum x1 -> x0, waiting for transfers between devices: 42.5 us -> none  [on_device(): probe_grad = lax.psum(probe_sum, 'rows')]
    all_to_all x6 -> x0, starting transfers between devices: 40.9 us -> none  [the longest x3 21.6 us: spectral_pass(): lax.all_to_all(returning, 'cols', split_axis=2, concat_axis=2, tiled=True)]
    dot_general x48 -> x0, matrix products: 39.2 us -> none  [the longest x12 15.8 us: fourth(): jnp.einsum('msub,sua->mba', values, matrix, preferred_element_type=jnp.fl...]
    reduce_scatter x1 -> x0, waiting for transfers between devices: 31.5 us -> none  [on_device(): summed = lax.psum_scatter(folded, 'rows', scatter_dimension=2, tiled=True)]
    another operation x7 -> x1, other arithmetic: 19.6 us -> 0.18 us  [the longest x3 9.71 us: spectral_pass(): outgoing = jnp.stack([first_real, first_imag], axis=1).astype(jnp.bfloat16)]
  transfers between devices with their start and end apart: 12 -> 0, of which waited for: 12 -> 0; matrix products, arithmetic and copies ran while one was open for 3% -> 0% of each run, Pallas kernels for 0% -> 0%
where the time goes in v1:
time: 200 us; the launch traced here: 197 us
  Pallas kernels  167 us (84%)
  other arithmetic  19.8 us (10%)
  local copies, waits for them, and re-layouts  9.12 us (5%)
    pallas_call x5, Pallas kernels, communicate(): pl.pallas_call(kernel, out_shape=[jax.ShapeDtypeStruct(shape, dtype) for...  127 us
    pallas_call x1, Pallas kernels, balanced_device(): pl.pallas_call(backward, grid_spec=pltpu.PrefetchScalarGridSpec(num_scala...  21 us
    pallas_call x1, Pallas kernels, balanced_device(): pl.pallas_call(forward, grid_spec=pltpu.PrefetchScalarGridSpec(num_scalar...  18.5 us

profile of v1, /device:TPU:9, one launch (start us, length us, event | category | flops | bytes accessed | tf_op | source)
XLA Modules:
  0.0 197.2 jit_solution(3486895271905204009)
XLA Ops:
  0.6 0.0 copy-start
  1.4 0.7 pad_add_fusion
  2.2 0.6 broadcast_in_dim.23.meta
  2.8 1.6 convert_element_type.35.cells
  4.4 0.0 copy-done
  4.4 0.7 fusion.probe
  5.1 2.4 %convert_element_type.36.frames = bf16[6,128,512]{2,1,0:T(8,128)(2,1)} convert(f32[6,128,512]{2,1,0:T(8,128)} %param.12) | non-fusion elementwise | flops 393216 | bytes 2359296 | tf_op jit(solution)/shard_map/convert_element_type | solution.py:518
  7.5 39.8 %spread_inputs.1 = (s32[4,8,128]{2,1,0:T(8,128)}, bf16[4,2,128,512]{3,2,1,0:T(8,128)(2,1)}, bf16[4,4,2,128,256]{4,3,2,1,0:T(8,128)(2,1)}, bf16[4,6,128,512]{3,2,1,0:T(8,128)(2,1)}) custom-call(s32[8,128]{1,0:T(8,128)} %broadcast_in_dim.23.meta, bf16[2,128,512]{2,1,0:T(8,128)(2,1)} %fusion.probe, bf16[2,128,256]{2,1,0:T(8,128)(2,1)} %convert_element_type.35.cells, ...), custom_call_target="tpu_custom_call" | custom-call | tf_op jit(solution)/shard_map/spread_inputs/pallas_call | solution.py:384
  47.3 0.9 slice_reduce_fusion.2
  48.2 0.9 slice_reduce_fusion
  49.1 0.1 reshape_squeeze.7
  49.2 0.2 reduce-window.8
  49.4 0.1 convert_reduce_fusion.2
  49.4 0.1 reshape_squeeze.6
  49.5 0.1 reduce_sum.57
  49.6 0.7 gather_fusion
  50.3 0.1 compare_select_fusion.2
  50.4 0.1 gather.18
  50.5 0.6 gather_fusion.3
  51.1 0.6 gather_fusion.2
  51.8 0.6 broadcast_select_fusion.1
  52.4 3.7 %gather_fusion.1 = bf16[12,128,512]{2,1,0:T(8,128)(2,1)} fusion(bf16[24,128,512]{2,1,0:T(8,128)(2,1)} %bitcast.29, s32[1024]{0:T(1024)S(1)} %pad_clamp_fusion), kind=kCustom, calls=%fused_computation.3 | custom fusion | bytes 3145776 | tf_op jit(solution)/shard_map/jit(_take)/gather | solution.py:532
  56.1 2.8 %broadcast_select_fusion.frames = bf16[4,3,128,512]{3,2,1,0:T(8,128)(2,1)} fusion(bf16[4,3,128,512]{3,2,1,0:T(8,128)(2,1)} %bitcast.28, pred[4,3]{1,0:T(4,128)(4,1)S(1)} %compare_and_fusion.1), kind=kLoop, calls=%fused_computation.5 | loop fusion | flops 786432 | bytes 3145740 | tf_op jit(solution)/shard_map/jit(_take)/select_n | solution.py:532
  58.9 18.5 %forward.1 = (bf16[3,2,512,512]{3,2,1,0:T(8,128)(2,1)}, f32[3,2,512,512]{3,2,1,0:T(8,128)}, bf16[4,3,128,512]{3,2,1,0:T(8,128)(2,1)}) custom-call(s32[3]{0:T(128)} %get-tuple-element.36.rows, s32[3]{0:T(128)} %get-tuple-element.35.cols, bf16[4,4,2,128,256]{4,3,2,1,0:T(8,128)(2,1)} %get-tuple-element.19.cells, ...), custom_call_target="tpu_custom_call" | custom-call | tf_op jit(solution)/shard_map/forward/pallas_call | solution.py:540
  77.5 25.3 %exchange_intensity.1 = (bf16[4,3,128,512]{3,2,1,0:T(8,128)(2,1)}, bf16[3,128,512]{2,1,0:T(8,128)(2,1)}) custom-call(bf16[4,3,128,512]{3,2,1,0:T(8,128)(2,1)} %get-tuple-element.21.intensity, bf16[4,3,128,512]{3,2,1,0:T(8,128)(2,1)} %broadcast_select_fusion.frames), custom_call_target="tpu_custom_call" | custom-call | tf_op jit(solution)/shard_map/exchange_intensity/pallas_call | solution.py:384
  102.8 0.0 copy-start.2
  102.8 1.8 convert_reduce_fusion
  104.6 0.0 copy-done.2
  104.6 0.9 subtract_convert_fusion.factor
  105.5 19.7 %gather_factors.1.factor = bf16[4,3,128,512]{3,2,1,0:T(8,128)(2,1)} custom-call(bf16[3,128,512]{2,1,0:T(8,128)(2,1)} %subtract_convert_fusion.factor), custom_call_target="tpu_custom_call" | custom-call | tf_op jit(solution)/shard_map/gather_factors/pallas_call | solution.py:384
  125.2 21.0 %backward.1 = (bf16[4,2,128,512]{3,2,1,0:T(8,128)(2,1)}, bf16[4,4,2,128,256]{4,3,2,1,0:T(8,128)(2,1)}) custom-call(s32[3]{0:T(128)} %get-tuple-element.36.rows, s32[3]{0:T(128)} %get-tuple-element.35.cols, bf16[4,3,128,512]{3,2,1,0:T(8,128)(2,1)} %gather_factors.1.factor, f32[3,2,512,512]{3,2,1,0:T(8,128)} %get-tuple-element.25.field, ...), custom_call_target="tpu_custom_call" | custom-call | tf_op jit(solution)/shard_map/backward/pallas_call | solution.py:568
  146.2 27.4 %scatter_gradients.1 = (bf16[4,2,128,512]{3,2,1,0:T(8,128)(2,1)}, bf16[4,4,2,128,256]{4,3,2,1,0:T(8,128)(2,1)}) custom-call(bf16[4,2,128,512]{3,2,1,0:T(8,128)(2,1)} %get-tuple-element.27.probe_grad, bf16[4,4,2,128,256]{4,3,2,1,0:T(8,128)(2,1)} %get-tuple-element.28.cells_grad), custom_call_target="tpu_custom_call" | custom-call | tf_op jit(solution)/shard_map/scatter_gradients/pallas_call | solution.py:384
  173.6 0.0 copy-start.1
  173.6 2.9 %reduce_sum.59.cells_grad = bf16[4,2,128,256]{3,2,1,0:T(8,128)(2,1)} reduce(bf16[4,4,2,128,256]{4,3,2,1,0:T(8,128)(2,1)} %get-tuple-element.29, bf16[]{:T(256)} %constant.76.clone.1), dimensions={0}, to_apply=%region_3.5 | reduce | flops 786432 | bytes 2621442 | tf_op jit(solution)/shard_map/reduce_sum | solution.py:596
  176.5 0.0 copy-done.1
  176.5 0.9 reduce_sum.60.probe_grad
  177.4 15.1 %finish_gradients.1 = (bf16[4,2,128,256]{3,2,1,0:T(8,128)(2,1)}, bf16[4,2,128,512]{3,2,1,0:T(8,128)(2,1)}) custom-call(bf16[4,2,128,256]{3,2,1,0:T(8,128)(2,1)} %reduce_sum.59.cells_grad, bf16[2,128,512]{2,1,0:T(8,128)(2,1)} %reduce_sum.60.probe_grad), custom_call_target="tpu_custom_call" | custom-call | tf_op jit(solution)/shard_map/finish_gradients/pallas_call | solution.py:384
  192.6 1.8 convert_reduce_fusion.1
  194.4 2.8 %convert_element_type.42 = f32[4,2,128,512]{3,2,1,0:T(8,128)} convert(bf16[4,2,128,512]{3,2,1,0:T(8,128)(2,1)} %get-tuple-element.32) | non-fusion elementwise | flops 524288 | bytes 3145728 | tf_op jit(solution)/shard_map/convert_element_type | solution.py:600
  (9 shorter events, 0.1 us)
Async XLA Ops:
  0.6 3.8 %copy-start = (f32[4,2,128,512]{3,2,1,0:T(8,128)S(1)}, f32[4,2,128,512]{3,2,1,0:T(8,128)}, u32[]{:S(2)}) copy-start(f32[4,2,128,512]{3,2,1,0:T(8,128)} %param.11) | copy-start | bytes 6291460
  102.8 1.8 copy-start.2
  173.6 3.0 %copy-start.1 = (bf16[4,2,128,512]{3,2,1,0:T(8,128)(2,1)S(1)}, bf16[4,2,128,512]{3,2,1,0:T(8,128)(2,1)}, u32[]{:S(2)}) copy-start(bf16[4,2,128,512]{3,2,1,0:T(8,128)(2,1)} %get-tuple-element.30) | copy-start | bytes 3145732

commit v2 on v1

--- a/solution.py
+++ b/solution.py
@@ -191,7 +191,9 @@
     indices = np.arange(length)
     angles = (indices[:, None] * indices[None, :] % length) * (2.0 * np.pi / length)
     scaling = 1.0 / length**0.5
-    return jnp.asarray(np.cos(angles) * scaling, jnp.bfloat16), jnp.asarray(np.sin(angles) * scaling, jnp.bfloat16)
+    cosine, sine = np.cos(angles) * scaling, np.sin(angles) * scaling
+    table = np.block([[cosine, -sine], [sine, cosine]])
+    return jnp.asarray(table, jnp.bfloat16), jnp.asarray(table.T, jnp.bfloat16)
 
 
 ANY = pl.BlockSpec(memory_space=pl.ANY)
@@ -321,39 +323,129 @@
             remote(frames, frames_out.at[row], sems, 12 + k, {"rows": lax.rem(row + k, N)}).wait_send()
 
 
-def exchange_intensity(intensity, frames, parts_out, frames_out, sems):
+def propagate(
+    patch, probe, frames, table, table_t, probe_out, terms, field, power, parts, scale, measured, wide, tall, total, sems
+):
     row, col = lax.axis_index("rows"), lax.axis_index("cols")
+    length = patch.shape[-1]
+    quarter = length // N
+    f32, bf16 = jnp.float32, jnp.bfloat16
     greet(("rows", "cols"))
-    parts = Gather("rows", intensity, parts_out, sems, 0, scatter=True)
-    parts.start()
+
+    def frame_copy(to):
+        return remote(frames.at[to], measured, sems, 18 + lax.rem(to + N - row, N), {"cols": to})
+
+    local_frames = pltpu.make_async_copy(frames.at[col], measured, sems.at[0, 18])
 
     @pl.when(row == col)
     def _():
-        local = pltpu.make_async_copy(frames.at[col], frames_out, sems.at[0, 4])
-        copies = []
-        for k in range(1, N):
-            to = lax.rem(col + k, N)
-            copies.append(remote(frames.at[to], frames_out, sems, 4 + k, {"cols": to}))
-            copies[-1].start()
-        local.start()
-        local.wait()
-        for copy in copies:
-            copy.wait_send()
-
-    for k in range(1, N):
-
-        @pl.when(lax.rem(row + k, N) == col)
+        local_frames.start()
+        for k in range(1, N):
+            frame_copy(lax.rem(col + k, N)).start()
+
+    def power_copy(p, k):
+        to = lax.rem(row + k, N)
+        return remote(power.at[p, to], parts.at[p, k - 1], sems, p * 3 + k - 1, {"rows": to})
+
+    def scale_copy(p, k, index):
+        to = lax.rem(row + k, N)
+        return remote(scale.at[p, index], scale.at[p, index], sems, 9 + p * 3 + k - 1, {"rows": to})
+
+    def factors(p):
+        for k in range(1, N):
+            power_copy(p, k).wait_recv()
+        intensity = power[p, row].astype(f32)
+        for k in range(1, N):
+            intensity += parts[p, k - 1].astype(f32)
+        amplitude = measured[p].astype(f32).T
+        scale[p, row] = (1.0 - amplitude * lax.rsqrt(jnp.maximum(intensity, 0.25))).astype(bf16)
+        for k in range(1, N):
+            scale_copy(p, k, row).start()
+
+    def transform(p, carry):
+        probe_real = probe[:, 0].reshape(length, length).astype(f32)
+        probe_imag = probe[:, 1].reshape(length, length).astype(f32)
+        patch_real = patch[p, 0].astype(f32)
+        patch_imag = patch[p, 1].astype(f32)
+        wide[:, :length] = (probe_real * patch_real - probe_imag * patch_imag).astype(bf16)
+        wide[:, length:] = (probe_real * patch_imag + probe_imag * patch_real).astype(bf16)
+        spread = mul(wide[...], table[...])
+        tall[:length] = spread[:, :length].astype(bf16)
+        tall[length:] = spread[:, length:].astype(bf16)
+        result = mul(table_t[...], tall[...])
+        field[p] = result
+        square = result[:length] * result[:length] + result[length:] * result[length:]
+        for q in range(N):
+            power[p, q] = square[:, q * quarter : (q + 1) * quarter].astype(bf16)
+        for k in range(1, N):
+            power_copy(p, k).start()
+
+        @pl.when(p == 1)
         def _():
-            remote(frames.at[col], frames_out, sems, 4 + k, {"cols": row}).wait_recv()
-
-    parts.wait()
-
-
-def gather_factors(factor, out, sems):
-    greet(("rows",))
-    job = Gather("rows", factor, out, sems, 0)
-    job.start()
-    job.wait()
+            @pl.when(row == col)
+            def _():
+                local_frames.wait()
+
+            for k in range(1, N):
+
+                @pl.when(lax.rem(row + k, N) == col)
+                def _():
+                    remote(measured, measured, sems, 18 + k, {"cols": row}).wait_recv()
+
+        @pl.when(p >= 1)
+        def _():
+            factors(p - 1)
+
+        return carry
+
+    lax.fori_loop(0, POS_AVG, transform, 0)
+    total[...] = jnp.zeros(total.shape, f32)
+
+    def back_transform(p, carry):
+        for k in range(1, N):
+            scale_copy(p, k, lax.rem(row + N - k, N)).wait_recv()
+        for q in range(N):
+            lanes = pl.ds(q * quarter, quarter)
+            gain = scale[p, q].astype(f32)
+            tall[:length, lanes] = (field[p, :length, lanes] * gain).astype(bf16)
+            tall[length:, lanes] = (field[p, length:, lanes] * gain).astype(bf16)
+        inner = mul(table[...], tall[...])
+        wide[:, :length] = inner[:length].astype(bf16)
+        wide[:, length:] = inner[length:].astype(bf16)
+        back = mul(wide[...], table_t[...])
+        back_real, back_imag = back[:, :length], back[:, length:]
+        probe_real = probe[:, 0].reshape(length, length).astype(f32)
+        probe_imag = probe[:, 1].reshape(length, length).astype(f32)
+        terms[p, 0] = probe_real * back_real + probe_imag * back_imag
+        terms[p, 1] = probe_real * back_imag - probe_imag * back_real
+        patch_real = patch[p, 0].astype(f32)
+        patch_imag = patch[p, 1].astype(f32)
+        total[0] += patch_real * back_real + patch_imag * back_imag
+        total[1] += patch_real * back_imag - patch_imag * back_real
+
+        @pl.when(p == 0)
+        def _():
+            factors(POS_AVG - 1)
+
+        return carry
+
+    lax.fori_loop(0, POS_AVG, back_transform, 0)
+    for b in range(N):
+        for part in range(2):
+            probe_out[b, part] = total[part, b * quarter : (b + 1) * quarter].astype(bf16)
+
+    def finish(p, carry):
+        for k in range(1, N):
+            power_copy(p, k).wait_send()
+            scale_copy(p, k, row).wait_send()
+        return carry
+
+    lax.fori_loop(0, POS_AVG, finish, 0)
+
+    @pl.when(row == col)
+    def _():
+        for k in range(1, N):
+            frame_copy(lax.rem(col + k, N)).wait_send()
 
 
 def scatter_gradients(probe_grad, cells_grad, probe_out, cells_out, sems):
@@ -396,14 +488,10 @@
     return jnp.dot(left, right, preferred_element_type=jnp.float32)
 
 
-def mul_t(left, right):
-    return lax.dot_general(left, right, (((1,), (1,)), ((), ())), preferred_element_type=jnp.float32)
-
-
-def forward(rows, cols, cells, probe, cosine, sine, patch_out, field_out, power_out, window):
+def cut(rows, cols, cells, patch_out, window):
     p = pl.program_id(0)
     strips, blocks, _, width, depth = cells.shape
-    length = cosine.shape[0]
+    length = patch_out.shape[-1]
     all_rows, all_cols = strips * depth, blocks * width
 
     @pl.when(p == 0)
@@ -421,71 +509,35 @@
     rest = lax.rem(first, 128)
     base = pl.multiple_of(first - rest, 128)
     span = length + 128
-    patch = []
+    tall = window.shape[1]
     for part in range(2):
         block = pltpu.roll(window[part, :, pl.ds(base, span)], lax.rem(span - rest, span), 1)[:, :length]
-        tall = window.shape[1]
-        patch.append(pltpu.roll(block, lax.rem(tall - cols[p], tall), 0)[:length])
-        patch_out[0, part] = patch[part].astype(jnp.bfloat16)
-    probe_real = probe[:, 0].reshape(length, length).astype(jnp.float32)
-    probe_imag = probe[:, 1].reshape(length, length).astype(jnp.float32)
-    wave_real = (probe_real * patch[0] - probe_imag * patch[1]).astype(jnp.bfloat16)
-    wave_imag = (probe_real * patch[1] + probe_imag * patch[0]).astype(jnp.bfloat16)
-    c, s = cosine[...], sine[...]
-    spread_real = (mul_t(c, wave_real) + mul_t(s, wave_imag)).astype(jnp.bfloat16)
-    spread_imag = (mul_t(c, wave_imag) - mul_t(s, wave_real)).astype(jnp.bfloat16)
-    field_real = mul(spread_real, c) + mul(spread_imag, s)
-    field_imag = mul(spread_imag, c) - mul(spread_real, s)
-    field_out[0, 0] = field_real
-    field_out[0, 1] = field_imag
-    power = field_real * field_real + field_imag * field_imag
-    power_out[:, 0] = power.reshape(N, length // N, length).astype(jnp.bfloat16)
-
-
-def backward(
-    rows, cols, factor, field, patch, probe, cosine, sine, probe_out, cells_out, window, total, padded
-):
+        block = pltpu.roll(block, lax.rem(tall - cols[p], tall), 0)[:length]
+        patch_out[0, part] = block.astype(jnp.bfloat16)
+
+
+def place(rows, cols, terms, cells_out, window, padded):
     p = pl.program_id(0)
     strips, blocks, _, width, depth = cells_out.shape
-    length = cosine.shape[0]
+    length = terms.shape[-1]
     span = length + 128
 
     @pl.when(p == 0)
     def _():
         window[...] = jnp.zeros(window.shape, jnp.float32)
-        total[...] = jnp.zeros(total.shape, jnp.float32)
         padded[...] = jnp.zeros(padded.shape, jnp.float32)
 
-    scale = factor[:, 0].reshape(length, length).astype(jnp.float32)
-    c, s = cosine[...], sine[...]
-    corrected_real = (field[0, 0] * scale).astype(jnp.bfloat16)
-    corrected_imag = (field[0, 1] * scale).astype(jnp.bfloat16)
-    inner_real = (mul_t(c, corrected_real) - mul_t(s, corrected_imag)).astype(jnp.bfloat16)
-    inner_imag = (mul_t(c, corrected_imag) + mul_t(s, corrected_real)).astype(jnp.bfloat16)
-    back_real = mul(inner_real, c) - mul(inner_imag, s)
-    back_imag = mul(inner_imag, c) + mul(inner_real, s)
-    patch_real = patch[0, 0].astype(jnp.float32)
-    patch_imag = patch[0, 1].astype(jnp.float32)
-    total[0] += patch_real * back_real + patch_imag * back_imag
-    total[1] += patch_real * back_imag - patch_imag * back_real
-    probe_real = probe[:, 0].reshape(length, length).astype(jnp.float32)
-    probe_imag = probe[:, 1].reshape(length, length).astype(jnp.float32)
     first = rows[p]
     rest = lax.rem(first, 128)
     base = pl.multiple_of(first - rest, 128)
     for part in range(2):
-        if part == 0:
-            term = probe_real * back_real + probe_imag * back_imag
-        else:
-            term = probe_real * back_imag - probe_imag * back_real
-        padded[:length, :length] = term
+        padded[:length, :length] = terms[0, part]
         window[part, :, pl.ds(base, span)] += pltpu.roll(pltpu.roll(padded[...], cols[p], 0), rest, 1)
 
     @pl.when(p == pl.num_programs(0) - 1)
     def _():
         for part in range(2):
             for b in range(blocks):
-                probe_out[b, part] = total[part, pl.ds(b * width, width), :].astype(jnp.bfloat16)
                 for s in range(strips):
                     cells_out[s, b, part] = window[part, pl.ds(b * width, width), pl.ds(s * depth, depth)].astype(
                         jnp.bfloat16
@@ -497,7 +549,7 @@
     width, depth = object_field.shape[1:]
     length = probe.shape[3]
     row, col = lax.axis_index("rows"), lax.axis_index("cols")
-    cosine, sine = tables(length)
+    table, table_t = tables(length)
     meta = jnp.concatenate([strip_counts, row_offsets, col_offsets])
     meta = jnp.pad(meta, (0, 128 - meta.shape[0]))[None, :]
     meta = jnp.broadcast_to(meta, (8, 128))
@@ -529,66 +581,62 @@
     my_strip = lax.dynamic_slice(strip_of, (col * POS_AVG,), (POS_AVG,))
     first_rows = my_strip * depth + jnp.take(rows_all, mine)
     first_cols = jnp.take(cols_all, mine)
-    frames = jnp.take(frames_all.reshape((-1,) + amplitudes.shape[1:]), slot, axis=0)
+    frames = jnp.take(frames_all.reshape((-1,) + amplitudes.shape[1:]), slot, axis=0, mode="clip")
     frames = frames.reshape((N, POS_AVG) + amplitudes.shape[1:])
 
     plane = (1, 2, length, length)
     whole = lambda *shape: pl.BlockSpec(shape, lambda p, *_: (0,) * len(shape))
     per_slot = pl.BlockSpec(plane, lambda p, *_: (p, 0, 0, 0))
-    quarters = pl.BlockSpec((N, 1, length // N, length), lambda p, *_: (0, p, 0, 0))
     window = pltpu.VMEM((2, N * width + 128, N * depth + length), f32)
-    patch, field, power = pl.pallas_call(
-        forward,
+    quarters = (POS_AVG, N, length, length // N)
+    patch = pl.pallas_call(
+        cut,
         grid_spec=pltpu.PrefetchScalarGridSpec(
             num_scalar_prefetch=2,
             grid=(POS_AVG,),
-            in_specs=[
-                whole(*cells.shape),
-                whole(*mode_all.shape),
-                whole(length, length),
-                whole(length, length),
-            ],
-            out_specs=[per_slot, per_slot, quarters],
+            in_specs=[whole(*cells.shape)],
+            out_specs=per_slot,
             scratch_shapes=[window],
         ),
+        out_shape=jax.ShapeDtypeStruct((POS_AVG,) + plane[1:], bf16),
+        compiler_params=pltpu.CompilerParams(vmem_limit_bytes=LIMIT),
+        name="cut",
+    )(first_rows, first_cols, cells)
+    probe_part, terms = pl.pallas_call(
+        propagate,
+        in_specs=[WHOLE, WHOLE, ANY, WHOLE, WHOLE],
+        out_specs=[WHOLE, WHOLE],
         out_shape=[
-            jax.ShapeDtypeStruct((POS_AVG,) + plane[1:], bf16),
+            jax.ShapeDtypeStruct(mode_all.shape, bf16),
             jax.ShapeDtypeStruct((POS_AVG,) + plane[1:], f32),
-            jax.ShapeDtypeStruct((N, POS_AVG, length // N, length), bf16),
         ],
-        compiler_params=pltpu.CompilerParams(vmem_limit_bytes=LIMIT),
-        name="forward",
-    )(first_rows, first_cols, cells, mode_all, cosine, sine)
-    powers, measured = communicate(
-        exchange_intensity, 2, 8, [(power.shape, bf16), (power.shape[1:], bf16)], power, frames
-    )
-    intensity = jnp.sum(powers.astype(f32), axis=0)
-    factor = 1.0 - measured.astype(f32) * lax.rsqrt(jnp.maximum(intensity, 0.25))
-    (factors,) = communicate(gather_factors, 3, 4, [(power.shape, bf16)], factor.astype(bf16))
-    probe_part, cells_part = pl.pallas_call(
-        backward,
+        scratch_shapes=[
+            pltpu.VMEM((POS_AVG, 2 * length, length), f32),
+            pltpu.VMEM(quarters, bf16),
+            pltpu.VMEM((POS_AVG, N - 1) + quarters[2:], bf16),
+            pltpu.VMEM(quarters, bf16),
+            pltpu.VMEM(frames.shape[1:], bf16),
+            pltpu.VMEM((length, 2 * length), bf16),
+            pltpu.VMEM((2 * length, length), bf16),
+            pltpu.VMEM((2, length, length), f32),
+            pltpu.SemaphoreType.DMA((2, 22)),
+        ],
+        compiler_params=pltpu.CompilerParams(collective_id=2, has_side_effects=True, vmem_limit_bytes=LIMIT),
+        name="propagate",
+    )(patch, mode_all, frames, table, table_t)
+    cells_part = pl.pallas_call(
+        place,
         grid_spec=pltpu.PrefetchScalarGridSpec(
             num_scalar_prefetch=2,
             grid=(POS_AVG,),
-            in_specs=[
-                quarters,
-                per_slot,
-                per_slot,
-                whole(*mode_all.shape),
-                whole(length, length),
-                whole(length, length),
-            ],
-            out_specs=[whole(*mode_all.shape), whole(*cells.shape)],
-            scratch_shapes=[
-                window,
-                pltpu.VMEM((2, length, length), f32),
-                pltpu.VMEM((window.shape[1], length + 128), f32),
-            ],
+            in_specs=[per_slot],
+            out_specs=whole(*cells.shape),
+            scratch_shapes=[window, pltpu.VMEM((window.shape[1], length + 128), f32)],
         ),
-        out_shape=[jax.ShapeDtypeStruct(mode_all.shape, bf16), jax.ShapeDtypeStruct(cells.shape, bf16)],
+        out_shape=jax.ShapeDtypeStruct(cells.shape, bf16),
         compiler_params=pltpu.CompilerParams(vmem_limit_bytes=LIMIT),
-        name="backward",
-    )(first_rows, first_cols, factors, field, patch, mode_all, cosine, sine)
+        name="place",
+    )(first_rows, first_cols, terms)
     probe_parts, cells_parts = communicate(
         scatter_gradients, 4, 8, [(probe_part.shape, bf16), (cells_part.shape, bf16)], probe_part, cells_part
     )

time: 200 us -> 183 us (0.915)
  Pallas kernels: 167 us -> 156 us
  other arithmetic: 19.8 us -> 14.3 us
    pallas_call x5 -> x3, Pallas kernels: 127 us -> 83.7 us  [communicate(): pl.pallas_call(kernel, out_shape=[jax.ShapeDtypeStruct(shape, dtype) for...]
    pallas_call x2 -> x3, Pallas kernels: 39.5 us -> 72.3 us  [the longest x1 49.7 us: balanced_device(): pl.pallas_call(propagate, in_specs=[WHOLE, WHOLE, ANY, WHOLE, WHOLE], out...]
    select_n x2 -> x0, other arithmetic: 2.81 us -> none  [balanced_device(): jnp.take(frames_all.reshape((-1,) + amplitudes.shape[1:]), slot, axis=0)]
where the time goes in v2:
time: 183 us; the launch traced here: 181 us
  Pallas kernels  156 us (85%)
  other arithmetic  14.3 us (8%)
  local copies, waits for them, and re-layouts  8.95 us (5%)
    pallas_call x3, Pallas kernels, communicate(): pl.pallas_call(kernel, out_shape=[jax.ShapeDtypeStruct(shape, dtype) for...  83.7 us
    pallas_call x1, Pallas kernels, balanced_device(): pl.pallas_call(propagate, in_specs=[WHOLE, WHOLE, ANY, WHOLE, WHOLE], out...  49.7 us
    pallas_call x1, Pallas kernels, balanced_device(): pl.pallas_call(place, grid_spec=pltpu.PrefetchScalarGridSpec(num_scalar_p...  11.8 us
    pallas_call x1, Pallas kernels, balanced_device(): pl.pallas_call(cut, grid_spec=pltpu.PrefetchScalarGridSpec(num_scalar_pre...  10.9 us
    gather x1, local copies, waits for them, and re-layouts, balanced_device(): jnp.take(frames_all.reshape((-1,) + amplitudes.shape[1:]), slot, axis=0,...  3.73 us

profile of v2, /device:TPU:9, one launch (start us, length us, event | category | flops | bytes accessed | tf_op | source)
XLA Modules:
  0.0 180.8 jit_solution(17731631788705187069)
XLA Ops:
  0.6 0.0 copy-start
  1.4 0.7 pad_add_fusion
  2.2 0.6 broadcast_in_dim.6.meta
  2.8 1.6 convert_element_type.26.cells
  4.4 0.0 copy-done
  4.4 0.7 fusion.probe
  5.1 2.4 %convert_element_type.27.frames = bf16[6,128,512]{2,1,0:T(8,128)(2,1)} convert(f32[6,128,512]{2,1,0:T(8,128)} %param.12) | non-fusion elementwise | flops 393216 | bytes 2359296 | tf_op jit(solution)/shard_map/convert_element_type | solution.py:570
  7.5 39.8 %spread_inputs.1 = (s32[4,8,128]{2,1,0:T(8,128)}, bf16[4,2,128,512]{3,2,1,0:T(8,128)(2,1)}, bf16[4,4,2,128,256]{4,3,2,1,0:T(8,128)(2,1)}, bf16[4,6,128,512]{3,2,1,0:T(8,128)(2,1)}) custom-call(s32[8,128]{1,0:T(8,128)} %broadcast_in_dim.6.meta, bf16[2,128,512]{2,1,0:T(8,128)(2,1)} %fusion.probe, bf16[2,128,256]{2,1,0:T(8,128)(2,1)} %convert_element_type.26.cells, ...), custom_call_target="tpu_custom_call" | custom-call | tf_op jit(solution)/shard_map/spread_inputs/pallas_call | solution.py:476
  47.3 0.9 slice_reduce_fusion.2
  48.2 0.9 slice_reduce_fusion
  49.1 0.1 reshape_squeeze.7
  49.2 0.2 reduce-window.8
  49.3 0.1 convert_reduce_fusion.1
  49.4 0.1 reshape_squeeze.6
  49.5 0.7 gather_fusion
  50.2 0.1 compare_select_fusion
  50.3 0.6 gather_fusion.3
  50.9 0.6 gather_fusion.2
  51.6 0.6 broadcast_select_fusion
  52.2 3.7 %gather_fusion.1 = bf16[12,128,512]{2,1,0:T(8,128)(2,1)} fusion(bf16[24,128,512]{2,1,0:T(8,128)(2,1)} %bitcast.29, s32[1024]{0:T(1024)S(1)} %pad_clamp_fusion), kind=kCustom, calls=%fused_computation.3 | custom fusion | bytes 3145776 | tf_op jit(solution)/shard_map/jit(_take)/gather | solution.py:584
  55.9 10.9 %cut.1.patch = bf16[3,2,512,512]{3,2,1,0:T(8,128)(2,1)} custom-call(s32[3]{0:T(128)} %get-tuple-element.26.rows, s32[3]{0:T(128)} %get-tuple-element.25.cols, bf16[4,4,2,128,256]{4,3,2,1,0:T(8,128)(2,1)} %get-tuple-element.14.cells), custom_call_target="tpu_custom_call" | custom-call | tf_op jit(solution)/shard_map/cut/pallas_call | solution.py:592
  66.8 49.7 %propagate.1 = (bf16[4,2,128,512]{3,2,1,0:T(8,128)(2,1)}, f32[3,2,512,512]{3,2,1,0:T(8,128)}) custom-call(bf16[3,2,512,512]{3,2,1,0:T(8,128)(2,1)} %cut.1.patch, bf16[4,2,128,512]{3,2,1,0:T(8,128)(2,1)} %get-tuple-element.15.probe, bf16[4,3,128,512]{3,2,1,0:T(8,128)(2,1)} %bitcast.28, bf16[1024,1024]{1,0:T(8,128)(2,1)} %constant.57.clone.table, ...), custom_call_target="tpu_custom_call" | custom-call | tf_op jit(solution)/shard_map/propagate/pallas_call | solution.py:605
  116.5 11.8 %place.1.cells_grad = bf16[4,4,2,128,256]{4,3,2,1,0:T(8,128)(2,1)} custom-call(s32[3]{0:T(128)} %get-tuple-element.26.rows, s32[3]{0:T(128)} %get-tuple-element.25.cols, f32[3,2,512,512]{3,2,1,0:T(8,128)} %get-tuple-element.18.terms), custom_call_target="tpu_custom_call" | custom-call | tf_op jit(solution)/shard_map/place/pallas_call | solution.py:627
  128.3 28.3 %scatter_gradients.1 = (bf16[4,2,128,512]{3,2,1,0:T(8,128)(2,1)}, bf16[4,4,2,128,256]{4,3,2,1,0:T(8,128)(2,1)}) custom-call(bf16[4,2,128,512]{3,2,1,0:T(8,128)(2,1)} %get-tuple-element.17.probe_grad, bf16[4,4,2,128,256]{4,3,2,1,0:T(8,128)(2,1)} %place.1.cells_grad), custom_call_target="tpu_custom_call" | custom-call | tf_op jit(solution)/shard_map/scatter_gradients/pallas_call | solution.py:476
  156.6 0.0 copy-start.1
  156.6 2.9 %reduce_sum.46.cells_grad = bf16[4,2,128,256]{3,2,1,0:T(8,128)(2,1)} reduce(bf16[4,4,2,128,256]{4,3,2,1,0:T(8,128)(2,1)} %get-tuple-element.19, bf16[]{:T(256)} %constant.55.clone.1), dimensions={0}, to_apply=%region_2.4 | reduce | flops 786432 | bytes 2621442 | tf_op jit(solution)/shard_map/reduce_sum | solution.py:644
  159.5 0.0 copy-done.1
  159.5 0.9 reduce_sum.47.probe_grad
  160.5 15.6 %finish_gradients.1 = (bf16[4,2,128,256]{3,2,1,0:T(8,128)(2,1)}, bf16[4,2,128,512]{3,2,1,0:T(8,128)(2,1)}) custom-call(bf16[4,2,128,256]{3,2,1,0:T(8,128)(2,1)} %reduce_sum.46.cells_grad, bf16[2,128,512]{2,1,0:T(8,128)(2,1)} %reduce_sum.47.probe_grad), custom_call_target="tpu_custom_call" | custom-call | tf_op jit(solution)/shard_map/finish_gradients/pallas_call | solution.py:476
  176.1 1.8 %convert_reduce_fusion = f32[2,128,256]{2,1,0:T(8,128)} fusion(bf16[4,2,128,256]{3,2,1,0:T(8,128)(2,1)} %get-tuple-element.21), kind=kLoop, calls=%fused_computation.4 | loop fusion | flops 458752 | bytes 786432 | tf_op jit(solution)/shard_map/reduce_sum | solution.py:648
  177.9 2.8 %convert_element_type.30 = f32[4,2,128,512]{3,2,1,0:T(8,128)} convert(bf16[4,2,128,512]{3,2,1,0:T(8,128)(2,1)} %get-tuple-element.22) | non-fusion elementwise | flops 524288 | bytes 3145728 | tf_op jit(solution)/shard_map/convert_element_type | solution.py:648
  (8 shorter events, 0.1 us)
Async XLA Ops:
  0.6 3.8 %copy-start = (f32[4,2,128,512]{3,2,1,0:T(8,128)S(1)}, f32[4,2,128,512]{3,2,1,0:T(8,128)}, u32[]{:S(2)}) copy-start(f32[4,2,128,512]{3,2,1,0:T(8,128)} %param.11) | copy-start | bytes 6291460
  156.6 3.0 %copy-start.1 = (bf16[4,2,128,512]{3,2,1,0:T(8,128)(2,1)S(1)}, bf16[4,2,128,512]{3,2,1,0:T(8,128)(2,1)}, u32[]{:S(2)}) copy-start(bf16[4,2,128,512]{3,2,1,0:T(8,128)(2,1)} %get-tuple-element.20) | copy-start | bytes 3145732

commit v3 on v2

--- a/solution.py
+++ b/solution.py
@@ -255,72 +255,151 @@
             copy.wait_send()
 
 
-def spread_inputs(meta, probe, cells, frames, meta_out, probe_out, cells_out, frames_out, sems):
+def spread_inputs(
+    meta, cells, probe, frames, meta_out, probe_out, cells_out, frames_out,
+    raw_probe, raw_frames, own_cells, own_probe, own_frames, sems, local
+):
+    bf16 = jnp.bfloat16
     row, col = lax.axis_index("rows"), lax.axis_index("cols")
     sibling = row + 1 - 2 * lax.rem(row, 2)
     across = lax.rem(row + 2, N)
+    opposite = lax.rem(sibling + 2, N)
+    right, left = lax.rem(col + 1, N), lax.rem(col + N - 1, N)
+    load_probe = pltpu.make_async_copy(probe.at[row], raw_probe, local.at[0])
+    load_frames = pltpu.make_async_copy(frames, raw_frames, local.at[1])
+    load_probe.start()
+    load_frames.start()
+    own_cells[...] = cells[...].astype(bf16)
     greet(("rows", "cols"))
-    blocks = Gather("cols", cells, cells_out.at[row], sems, 0)
-    blocks.start()
-    small = Gather("rows", meta, meta_out, sems, 4)
+
+    def line_copy(base, src, dst, origin, rightward):
+        return pltpu.make_async_remote_copy(
+            src_ref=src,
+            dst_ref=dst,
+            send_sem=sems.at[0 if rightward else 2, base + origin],
+            recv_sem=sems.at[1, base + origin],
+            device_id={"cols": right if rightward else left},
+            device_id_type=pl.DeviceIdType.MESH,
+        )
+
+    def line_start(base, src, dst, origin, rightward):
+        @pl.when(col < N - 1 if rightward else col > 0)
+        def _():
+            line_copy(base, src, dst, origin, rightward).start()
+
+    def line_sent(base, src, dst, origin, rightward):
+        @pl.when(col < N - 1 if rightward else col > 0)
+        def _():
+            line_copy(base, src, dst, origin, rightward).wait_send()
+
+    def cell(index, origin):
+        return cells_out.at[index, origin]
+
+    def row_copy(slot, src, dst, to):
+        return remote(src, dst, sems, slot, {"rows": to})
+
+    for rightward in (True, False):
+        line_start(0, own_cells, cell(row, col), col, rightward)
+    small = Gather("rows", meta, meta_out, sems, 8)
     small.start()
-    modes = Gather("cols", probe, probe_out, sems, 8)
-    modes.start()
-    local_frames = pltpu.make_async_copy(frames, frames_out.at[row], sems.at[0, 12])
+    row_copy(16 + col, own_cells, cell(row, col), across).start()
+    row_copy(20 + col, own_cells, cell(row, col), sibling).start()
+    keep_cells = pltpu.make_async_copy(own_cells, cell(row, col), local.at[2])
+    keep_cells.start()
+    load_probe.wait()
+    own_probe[...] = raw_probe[...].astype(bf16)
+    for rightward in (True, False):
+        line_start(4, own_probe, probe_out.at[col], col, rightward)
+    keep_probe = pltpu.make_async_copy(own_probe, probe_out.at[col], local.at[3])
+    keep_probe.start()
+    load_frames.wait()
+    own_frames[...] = raw_frames[...].astype(bf16)
+    keep_frames = pltpu.make_async_copy(own_frames, frames_out.at[row], local.at[4])
 
     @pl.when(row == col)
     def _():
-        local_frames.start()
+        keep_frames.start()
+
+    def frame_copy(k):
+        return row_copy(12 + k, own_frames, frames_out.at[row], lax.rem(row + k, N))
 
     for k in range(1, N):
 
         @pl.when(lax.rem(row + k, N) == col)
         def _():
-            remote(frames, frames_out.at[row], sems, 12 + k, {"rows": lax.rem(row + k, N)}).start()
-
-    started = []
-    for k in range(N):
-        source = lax.rem(col + N - k, N)
-        mine = cells_out.at[row, source]
-        if k == 0:
-            blocks.local.wait()
-        else:
-            remote(cells, mine, sems, k, {"cols": source}).wait_recv()
-        for slot, to in ((16 + k, across), (20 + k, sibling)):
-            copy = remote(mine, mine, sems, slot, {"rows": to})
-            copy.start()
-            started.append(copy)
-    for k in range(N):
-        source = lax.rem(col + N - k, N)
-        landed = cells_out.at[across, source]
-        remote(landed, landed, sems, 16 + k, {"rows": across}).wait_recv()
-        copy = remote(landed, landed, sems, 24 + k, {"rows": sibling})
-        copy.start()
-        started.append(copy)
-    opposite = lax.rem(sibling + 2, N)
-    for k in range(N):
-        source = lax.rem(col + N - k, N)
-        near = cells_out.at[sibling, source]
-        remote(near, near, sems, 20 + k, {"rows": sibling}).wait_recv()
-        far = cells_out.at[opposite, source]
-        remote(far, far, sems, 24 + k, {"rows": sibling}).wait_recv()
-    for copy in started + blocks.sent:
-        copy.wait_send()
+            frame_copy(k).start()
+
+    def from_side(d, rightward):
+        if rightward:
+            return col >= d, lax.rem(col + N - d, N)
+        return col + d < N, lax.rem(col + d, N)
+
+    for d in range(1, N):
+        for rightward in (True, False):
+            here, origin = from_side(d, rightward)
+
+            @pl.when(here)
+            def _():
+                mine = cell(row, origin)
+                line_copy(0, mine, mine, origin, rightward).wait_recv()
+                line_start(0, mine, mine, origin, rightward)
+                row_copy(16 + origin, mine, mine, across).start()
+                row_copy(20 + origin, mine, mine, sibling).start()
+
+        for rightward in (True, False):
+            here, origin = from_side(d, rightward)
+
+            @pl.when(here)
+            def _():
+                mine = probe_out.at[origin]
+                line_copy(4, mine, mine, origin, rightward).wait_recv()
+                line_start(4, mine, mine, origin, rightward)
+
+        if d == 1:
+            landed = cell(across, col)
+            row_copy(16 + col, landed, landed, across).wait_recv()
+            row_copy(24 + col, landed, landed, sibling).start()
+    for k in range(1, N):
+        origin = lax.rem(col + k, N)
+        landed = cell(across, origin)
+        row_copy(16 + origin, landed, landed, across).wait_recv()
+        row_copy(24 + origin, landed, landed, sibling).start()
+    for origin in range(N):
+        near, far = cell(sibling, origin), cell(opposite, origin)
+        row_copy(20 + origin, near, near, sibling).wait_recv()
+        row_copy(24 + origin, far, far, sibling).wait_recv()
+    keep_cells.wait()
+    keep_probe.wait()
+    for rightward in (True, False):
+        line_sent(0, own_cells, cell(row, col), col, rightward)
+        line_sent(4, own_probe, probe_out.at[col], col, rightward)
+        for d in range(1, N):
+            here, origin = from_side(d, rightward)
+
+            @pl.when(here)
+            def _():
+                line_sent(0, cell(row, origin), cell(row, origin), origin, rightward)
+                line_sent(4, probe_out.at[origin], probe_out.at[origin], origin, rightward)
+
+    for origin in range(N):
+        mine, landed = cell(row, origin), cell(across, origin)
+        row_copy(16 + origin, mine, mine, across).wait_send()
+        row_copy(20 + origin, mine, mine, sibling).wait_send()
+        row_copy(24 + origin, landed, landed, sibling).wait_send()
     small.wait()
-    modes.wait()
 
     @pl.when(row == col)
     def _():
-        local_frames.wait()
+        keep_frames.wait()
         for k in range(1, N):
             source = lax.rem(row + N - k, N)
-            remote(frames, frames_out.at[source], sems, 12 + k, {"rows": source}).wait_recv()
+            row_copy(12 + k, own_frames, frames_out.at[source], source).wait_recv()
 
     for k in range(1, N):
 
         @pl.when(lax.rem(row + k, N) == col)
         def _():
-            remote(frames, frames_out.at[row], sems, 12 + k, {"rows": lax.rem(row + k, N)}).wait_send()
+            frame_copy(k).wait_send()
 
 
 def propagate(
@@ -488,14 +567,42 @@
     return jnp.dot(left, right, preferred_element_type=jnp.float32)
 
 
-def cut(rows, cols, cells, patch_out, window):
+def locate(meta, position, depth):
+    strip, slot, start = 0, 0, 0
+    for s in range(N):
+        count = meta[s, 0, 0]
+        inside = (position >= start) & (position < start + count)
+        strip = jnp.where(inside, s, strip)
+        slot = jnp.where(inside, position - start, slot)
+        start = start + count
+    return strip, slot, strip * depth + meta[strip, 0, 1 + slot], meta[strip, 0, 1 + POS_MAX + slot]
+
+
+def iota(shape, axis):
+    return lax.broadcasted_iota(jnp.int32, shape, axis)
+
+
+def cut(meta, cells, frames_all, patch_out, frames_out, window, sems):
     p = pl.program_id(0)
     strips, blocks, _, width, depth = cells.shape
     length = patch_out.shape[-1]
     all_rows, all_cols = strips * depth, blocks * width
 
+    def frame_copies():
+        copies = []
+        for i in range(POS_AVG * N):
+            strip, slot, _, _ = locate(meta, i, depth)
+            copies.append(
+                pltpu.make_async_copy(
+                    frames_all.at[strip, slot], frames_out.at[i // POS_AVG, i % POS_AVG], sems.at[i]
+                )
+            )
+        return copies
+
     @pl.when(p == 0)
     def _():
+        for copy in frame_copies():
+            copy.start()
         for part, fill in ((0, 1.0), (1, 0.0)):
             window[part, all_cols:, :] = jnp.full((width, window.shape[2]), fill, jnp.float32)
             window[part, :all_cols, all_rows:] = jnp.full((all_cols, length), fill, jnp.float32)
@@ -505,34 +612,61 @@
                         jnp.float32
                     )
 
-    first = rows[p]
+    _, _, first, column = locate(meta, lax.axis_index("cols") * POS_AVG + p, depth)
     rest = lax.rem(first, 128)
-    base = pl.multiple_of(first - rest, 128)
-    span = length + 128
-    tall = window.shape[1]
+    base = first - rest
+    low = lax.rem(column, 8)
+    top = pl.multiple_of(column - low, 8)
+    groups = length // 8
     for part in range(2):
-        block = pltpu.roll(window[part, :, pl.ds(base, span)], lax.rem(span - rest, span), 1)[:, :length]
-        block = pltpu.roll(block, lax.rem(tall - cols[p], tall), 0)[:length]
-        patch_out[0, part] = block.astype(jnp.bfloat16)
-
-
-def place(rows, cols, terms, cells_out, window, padded):
+        before = None
+        for j in range(length // 128 + 1):
+            block = window[part, pl.ds(top, length + 8), pl.ds(pl.multiple_of(base + 128 * j, 128), 128)]
+            block = pltpu.roll(block.reshape(groups + 1, 8, 128), lax.rem(8 - low, 8), 1)
+            block = jnp.where(iota((groups, 8, 128), 1) < 8 - low, block[:groups], block[1:])
+            block = pltpu.roll(block.reshape(length, 128), lax.rem(128 - rest, 128), 1)
+            if j > 0:
+                joined = jnp.where(iota((length, 128), 1) < 128 - rest, before, block)
+                patch_out[0, part, :, 128 * (j - 1) : 128 * j] = joined.astype(jnp.bfloat16)
+            before = block
+
+    @pl.when(p == pl.num_programs(0) - 1)
+    def _():
+        for copy in frame_copies():
+            copy.wait()
+
+
+def place(meta, terms, cells_out, window):
     p = pl.program_id(0)
     strips, blocks, _, width, depth = cells_out.shape
     length = terms.shape[-1]
-    span = length + 128
 
     @pl.when(p == 0)
     def _():
         window[...] = jnp.zeros(window.shape, jnp.float32)
-        padded[...] = jnp.zeros(padded.shape, jnp.float32)
-
-    first = rows[p]
+
+    _, _, first, column = locate(meta, lax.axis_index("cols") * POS_AVG + p, depth)
     rest = lax.rem(first, 128)
-    base = pl.multiple_of(first - rest, 128)
+    base = first - rest
+    low = lax.rem(column, 8)
+    top = pl.multiple_of(column - low, 8)
+    groups = length // 8
+    edge = jnp.zeros((1, 8, 128), jnp.float32)
     for part in range(2):
-        padded[:length, :length] = terms[0, part]
-        window[part, :, pl.ds(base, span)] += pltpu.roll(pltpu.roll(padded[...], cols[p], 0), rest, 1)
+        before = jnp.zeros((length + 8, 128), jnp.float32)
+        for j in range(length // 128 + 1):
+            if j < length // 128:
+                block = terms[0, part, :, 128 * j : 128 * (j + 1)].reshape(groups, 8, 128)
+                block = pltpu.roll(block, low, 1)
+                above = jnp.concatenate([edge, block], axis=0)
+                below = jnp.concatenate([block, edge], axis=0)
+                block = jnp.where(iota((groups + 1, 8, 128), 1) < low, above, below)
+                block = pltpu.roll(block.reshape(length + 8, 128), rest, 1)
+            else:
+                block = jnp.zeros((length + 8, 128), jnp.float32)
+            joined = jnp.where(iota((length + 8, 128), 1) < rest, before, block)
+            window[part, pl.ds(top, length + 8), pl.ds(pl.multiple_of(base + 128 * j, 128), 128)] += joined
+            before = block
 
     @pl.when(p == pl.num_programs(0) - 1)
     def _():
@@ -552,56 +686,49 @@
     table, table_t = tables(length)
     meta = jnp.concatenate([strip_counts, row_offsets, col_offsets])
     meta = jnp.pad(meta, (0, 128 - meta.shape[0]))[None, :]
-    meta = jnp.broadcast_to(meta, (8, 128))
-    mode = lax.dynamic_index_in_dim(probe, row, 0, keepdims=False).astype(bf16)
-    meta_all, mode_all, cells, frames_all = communicate(
+    mode_shape = probe.shape[1:]
+    meta_all, mode_all, cells, frames_all = pl.pallas_call(
         spread_inputs,
-        1,
-        28,
-        [
-            ((N, 8, 128), jnp.int32),
-            ((N,) + mode.shape, bf16),
-            ((N, N) + object_field.shape, bf16),
-            ((N,) + amplitudes.shape, bf16),
+        in_specs=[ANY, WHOLE, ANY, ANY],
+        out_specs=[ANY] * 4,
+        out_shape=[
+            jax.ShapeDtypeStruct((N, 1, 128), jnp.int32),
+            jax.ShapeDtypeStruct((N,) + mode_shape, bf16),
+            jax.ShapeDtypeStruct((N, N) + object_field.shape, bf16),
+            jax.ShapeDtypeStruct((N,) + amplitudes.shape, bf16),
         ],
-        meta,
-        mode,
-        object_field.astype(bf16),
-        amplitudes.astype(bf16),
-    )
-    counts = meta_all[:, 0, 0]
-    totals = jnp.cumsum(counts)
-    starts = totals - counts
-    ids = jnp.arange(POS_AVG * N, dtype=jnp.int32)
-    strip_of = jnp.sum((totals[None, :] <= ids[:, None]).astype(jnp.int32), axis=1)
-    slot = strip_of * POS_MAX + ids - jnp.take(starts, strip_of)
-    rows_all = meta_all[:, 0, 1 : 1 + POS_MAX].reshape(-1)
-    cols_all = meta_all[:, 0, 1 + POS_MAX : 1 + 2 * POS_MAX].reshape(-1)
-    mine = lax.dynamic_slice(slot, (col * POS_AVG,), (POS_AVG,))
-    my_strip = lax.dynamic_slice(strip_of, (col * POS_AVG,), (POS_AVG,))
-    first_rows = my_strip * depth + jnp.take(rows_all, mine)
-    first_cols = jnp.take(cols_all, mine)
-    frames = jnp.take(frames_all.reshape((-1,) + amplitudes.shape[1:]), slot, axis=0, mode="clip")
-    frames = frames.reshape((N, POS_AVG) + amplitudes.shape[1:])
+        scratch_shapes=[
+            pltpu.VMEM(mode_shape, f32),
+            pltpu.VMEM(amplitudes.shape, f32),
+            pltpu.VMEM(object_field.shape, bf16),
+            pltpu.VMEM(mode_shape, bf16),
+            pltpu.VMEM(amplitudes.shape, bf16),
+            pltpu.SemaphoreType.DMA((3, 28)),
+            pltpu.SemaphoreType.DMA((5,)),
+        ],
+        compiler_params=pltpu.CompilerParams(collective_id=1, has_side_effects=True, vmem_limit_bytes=LIMIT),
+        name="spread_inputs",
+    )(meta, object_field, probe, amplitudes)
 
     plane = (1, 2, length, length)
-    whole = lambda *shape: pl.BlockSpec(shape, lambda p, *_: (0,) * len(shape))
-    per_slot = pl.BlockSpec(plane, lambda p, *_: (p, 0, 0, 0))
+    whole = lambda *shape: pl.BlockSpec(shape, lambda p: (0,) * len(shape))
+    per_slot = pl.BlockSpec(plane, lambda p: (p, 0, 0, 0))
+    scalars = pl.BlockSpec(memory_space=pltpu.SMEM)
     window = pltpu.VMEM((2, N * width + 128, N * depth + length), f32)
     quarters = (POS_AVG, N, length, length // N)
-    patch = pl.pallas_call(
+    patch, frames = pl.pallas_call(
         cut,
-        grid_spec=pltpu.PrefetchScalarGridSpec(
-            num_scalar_prefetch=2,
-            grid=(POS_AVG,),
-            in_specs=[whole(*cells.shape)],
-            out_specs=per_slot,
-            scratch_shapes=[window],
-        ),
-        out_shape=jax.ShapeDtypeStruct((POS_AVG,) + plane[1:], bf16),
+        grid=(POS_AVG,),
+        in_specs=[scalars, whole(*cells.shape), ANY],
+        out_specs=[per_slot, ANY],
+        scratch_shapes=[window, pltpu.SemaphoreType.DMA((POS_AVG * N,))],
+        out_shape=[
+            jax.ShapeDtypeStruct((POS_AVG,) + plane[1:], bf16),
+            jax.ShapeDtypeStruct((N, POS_AVG) + amplitudes.shape[1:], bf16),
+        ],
         compiler_params=pltpu.CompilerParams(vmem_limit_bytes=LIMIT),
         name="cut",
-    )(first_rows, first_cols, cells)
+    )(meta_all, cells, frames_all)
     probe_part, terms = pl.pallas_call(
         propagate,
         in_specs=[WHOLE, WHOLE, ANY, WHOLE, WHOLE],
@@ -626,17 +753,14 @@
     )(patch, mode_all, frames, table, table_t)
     cells_part = pl.pallas_call(
         place,
-        grid_spec=pltpu.PrefetchScalarGridSpec(
-            num_scalar_prefetch=2,
-            grid=(POS_AVG,),
-            in_specs=[per_slot],
-            out_specs=whole(*cells.shape),
-            scratch_shapes=[window, pltpu.VMEM((window.shape[1], length + 128), f32)],
-        ),
+        grid=(POS_AVG,),
+        in_specs=[scalars, per_slot],
+        out_specs=whole(*cells.shape),
+        scratch_shapes=[window],
         out_shape=jax.ShapeDtypeStruct(cells.shape, bf16),
         compiler_params=pltpu.CompilerParams(vmem_limit_bytes=LIMIT),
         name="place",
-    )(first_rows, first_cols, terms)
+    )(meta_all, terms)
     probe_parts, cells_parts = communicate(
         scatter_gradients, 4, 8, [(probe_part.shape, bf16), (cells_part.shape, bf16)], probe_part, cells_part
     )

time: 183 us -> 201 us (1.098)
  Pallas kernels: 156 us -> 188 us
  local copies, waits for them, and re-layouts: 8.95 us -> 0.52 us
  other arithmetic: 14.3 us -> 9.27 us
    pallas_call x2 -> x3, Pallas kernels: 22.6 us -> 95.2 us  [the longest x1 51.6 us: balanced_device(): pl.pallas_call(cut, grid=(POS_AVG,), in_specs=[scalars, whole(*cells.shap...]
    pallas_call x3 -> x2, Pallas kernels: 83.7 us -> 43.1 us  [communicate(): pl.pallas_call(kernel, out_shape=[jax.ShapeDtypeStruct(shape, dtype) for...]
    gather x4 -> x0, local copies, waits for them, and re-layouts: 5.67 us -> none  [the longest x1 3.73 us: balanced_device(): jnp.take(frames_all.reshape((-1,) + amplitudes.shape[1:]), slot, axis=0,...]
    convert_element_type x2 -> x0, other arithmetic: 3.99 us -> none  [the longest x1 2.39 us: balanced_device(): amplitudes.astype(bf16)]
where the time goes in v3:
time: 201 us; the launch traced here: 199 us
  Pallas kernels  188 us (94%)
  other arithmetic  9.27 us (5%)
    pallas_call x1, Pallas kernels, balanced_device(): pl.pallas_call(cut, grid=(POS_AVG,), in_specs=[scalars, whole(*cells.shap...  51.6 us
    pallas_call x1, Pallas kernels, balanced_device(): pl.pallas_call(propagate, in_specs=[WHOLE, WHOLE, ANY, WHOLE, WHOLE], out...  49.9 us
    pallas_call x2, Pallas kernels, communicate(): pl.pallas_call(kernel, out_shape=[jax.ShapeDtypeStruct(shape, dtype) for...  43.1 us
    pallas_call x1, Pallas kernels, balanced_device(): pl.pallas_call(spread_inputs, in_specs=[ANY, WHOLE, ANY, ANY], out_specs=...  36.8 us
    pallas_call x1, Pallas kernels, balanced_device(): pl.pallas_call(place, grid=(POS_AVG,), in_specs=[scalars, per_slot], out_...  6.81 us

profile of v3, /device:TPU:9, one launch (start us, length us, event | category | flops | bytes accessed | tf_op | source)
XLA Modules:
  0.0 199.3 jit_solution(15523496903642533427)
XLA Ops:
  1.3 0.7 pad_add_fusion
  2.0 0.5 pad_bitcast_fusion.meta
  2.5 36.8 %spread_inputs.1 = (s32[4,1,128]{2,1,0:T(1,128)}, bf16[4,2,128,512]{3,2,1,0:T(8,128)(2,1)}, bf16[4,4,2,128,256]{4,3,2,1,0:T(8,128)(2,1)}, bf16[4,6,128,512]{3,2,1,0:T(8,128)(2,1)}) custom-call(s32[1,128]{1,0:T(1,128)} %pad_bitcast_fusion.meta, f32[2,128,256]{2,1,0:T(8,128)} %cells.1, f32[4,2,128,512]{3,2,1,0:T(8,128)} %probe.1, f32[6,128,512]{2,1,0:T(8,128)} %frames.1), custom_call_target="tpu_custom_call" | custom-call | tf_op jit(solution)/shard_map/spread_inputs/pallas_call | solution.py:690
  39.3 51.6 %cut.1 = (bf16[3,2,512,512]{3,2,1,0:T(8,128)(2,1)}, bf16[4,3,128,512]{3,2,1,0:T(8,128)(2,1)}) custom-call(s32[4,1,128]{2,1,0:T(1,128)} %get-tuple-element.14.meta, bf16[4,4,2,128,256]{4,3,2,1,0:T(8,128)(2,1)} %get-tuple-element.15.cells, bf16[4,6,128,512]{3,2,1,0:T(8,128)(2,1)} %get-tuple-element.16.frames_all), custom_call_target="tpu_custom_call" | custom-call | tf_op jit(solution)/shard_map/cut/pallas_call | solution.py:719
  90.9 49.9 %propagate.1 = (bf16[4,2,128,512]{3,2,1,0:T(8,128)(2,1)}, f32[3,2,512,512]{3,2,1,0:T(8,128)}) custom-call(bf16[3,2,512,512]{3,2,1,0:T(8,128)(2,1)} %get-tuple-element.17.patch, bf16[4,2,128,512]{3,2,1,0:T(8,128)(2,1)} %get-tuple-element.18.probe, bf16[4,3,128,512]{3,2,1,0:T(8,128)(2,1)} %get-tuple-element.19.frames, ...), custom_call_target="tpu_custom_call" | custom-call | tf_op jit(solution)/shard_map/propagate/pallas_call | solution.py:732
  140.8 6.8 %place.1.cells_grad = bf16[4,4,2,128,256]{4,3,2,1,0:T(8,128)(2,1)} custom-call(s32[4,1,128]{2,1,0:T(1,128)} %get-tuple-element.14.meta, f32[3,2,512,512]{3,2,1,0:T(8,128)} %get-tuple-element.21.terms), custom_call_target="tpu_custom_call" | custom-call | tf_op jit(solution)/shard_map/place/pallas_call | solution.py:754
  147.6 27.7 %scatter_gradients.1 = (bf16[4,2,128,512]{3,2,1,0:T(8,128)(2,1)}, bf16[4,4,2,128,256]{4,3,2,1,0:T(8,128)(2,1)}) custom-call(bf16[4,2,128,512]{3,2,1,0:T(8,128)(2,1)} %get-tuple-element.20.probe_grad, bf16[4,4,2,128,256]{4,3,2,1,0:T(8,128)(2,1)} %place.1.cells_grad), custom_call_target="tpu_custom_call" | custom-call | tf_op jit(solution)/shard_map/scatter_gradients/pallas_call | solution.py:555
  175.4 0.0 copy-start
  175.4 2.9 %reduce_sum.33.cells_grad = bf16[4,2,128,256]{3,2,1,0:T(8,128)(2,1)} reduce(bf16[4,4,2,128,256]{4,3,2,1,0:T(8,128)(2,1)} %get-tuple-element.22, bf16[]{:T(256)} %constant.9.clone.1), dimensions={0}, to_apply=%region_0.1 | reduce | flops 786432 | bytes 2621442 | tf_op jit(solution)/shard_map/reduce_sum | solution.py:768
  178.3 0.0 copy-done
  178.3 0.9 reduce_sum.34.probe_grad
  179.2 15.4 %finish_gradients.1 = (bf16[4,2,128,256]{3,2,1,0:T(8,128)(2,1)}, bf16[4,2,128,512]{3,2,1,0:T(8,128)(2,1)}) custom-call(bf16[4,2,128,256]{3,2,1,0:T(8,128)(2,1)} %reduce_sum.33.cells_grad, bf16[2,128,512]{2,1,0:T(8,128)(2,1)} %reduce_sum.34.probe_grad), custom_call_target="tpu_custom_call" | custom-call | tf_op jit(solution)/shard_map/finish_gradients/pallas_call | solution.py:555
  194.6 1.8 convert_reduce_fusion
  196.4 2.8 %convert_element_type.5 = f32[4,2,128,512]{3,2,1,0:T(8,128)} convert(bf16[4,2,128,512]{3,2,1,0:T(8,128)(2,1)} %get-tuple-element.25) | non-fusion elementwise | flops 524288 | bytes 3145728 | tf_op jit(solution)/shard_map/convert_element_type | solution.py:772
Async XLA Ops:
  175.4 3.0 %copy-start = (bf16[4,2,128,512]{3,2,1,0:T(8,128)(2,1)S(1)}, bf16[4,2,128,512]{3,2,1,0:T(8,128)(2,1)}, u32[]{:S(2)}) copy-start(bf16[4,2,128,512]{3,2,1,0:T(8,128)(2,1)} %get-tuple-element.23) | copy-start | bytes 3145732

commit v4 on v3

--- a/solution.py
+++ b/solution.py
@@ -1,5 +1,3 @@
-import functools
-
 import jax
 import jax.numpy as jnp
 import numpy as np
@@ -527,40 +525,84 @@
             frame_copy(lax.rem(col + k, N)).wait_send()
 
 
-def scatter_gradients(probe_grad, cells_grad, probe_out, cells_out, sems):
+def reduce_gradients(
+    probe_part, cells_part, cells_out, probe_out, probe_in, near, far, relay, outgoing, cells_in, probe_all, sems
+):
+    f32, bf16 = jnp.float32, jnp.bfloat16
+    row, col = lax.axis_index("rows"), lax.axis_index("cols")
+    sibling = row + 1 - 2 * lax.rem(row, 2)
+    across = lax.rem(row + 2, N)
+    opposite = lax.rem(sibling + 2, N)
     greet(("rows", "cols"))
-    jobs = [
-        Gather("cols", probe_grad, probe_out, sems, 0, scatter=True),
-        Gather("rows", cells_grad, cells_out, sems, 4, scatter=True),
-    ]
-    for job in jobs:
-        job.start()
-    for job in jobs:
-        job.wait()
-
-
-def finish_gradients(cells_grad, probe_grad, cells_out, probe_out, sems):
-    greet(("rows", "cols"))
-    jobs = [
-        Gather("cols", cells_grad, cells_out, sems, 0, scatter=True),
-        Gather("rows", probe_grad, probe_out, sems, 4),
-    ]
-    for job in jobs:
-        job.start()
-    for job in jobs:
-        job.wait()
-
-
-def communicate(kernel, number, slots, outs, *args):
-    return pl.pallas_call(
-        kernel,
-        out_shape=[jax.ShapeDtypeStruct(shape, dtype) for shape, dtype in outs],
-        in_specs=[ANY] * len(args),
-        out_specs=[ANY] * len(outs),
-        scratch_shapes=[pltpu.SemaphoreType.DMA((2, slots))],
-        compiler_params=pltpu.CompilerParams(collective_id=number, has_side_effects=True),
-        name=kernel.__name__,
-    )(*args)
+
+    def probe_copy(k):
+        to = lax.rem(col + k, N)
+        return remote(probe_part.at[to], probe_in.at[k - 1], sems, k - 1, {"cols": to})
+
+    def near_copy(half, k):
+        b = lax.rem(col + k, N)
+        strip = opposite if half else sibling
+        return remote(cells_part.at[strip, b], near.at[half, b], sems, 3 + 4 * half + k, {"rows": sibling})
+
+    def far_copy(k):
+        b = lax.rem(col + k, N)
+        return remote(relay.at[b], far.at[b], sems, 11 + k, {"rows": across})
+
+    def cells_copy(k):
+        b = lax.rem(col + k, N)
+        return remote(outgoing.at[b], cells_in.at[k - 1], sems, 14 + k, {"cols": b})
+
+    def mode_copy(slot, index, to):
+        return remote(probe_all.at[index], probe_all.at[index], sems, slot, {"rows": to})
+
+    order = (1, 2, 3, 0)
+    for k in range(1, N):
+        probe_copy(k).start()
+    for half in (1, 0):
+        for k in order:
+            near_copy(half, k).start()
+    for k in order:
+        b = lax.rem(col + k, N)
+        near_copy(1, k).wait_recv()
+        relay[b] = (cells_part[across, b].astype(f32) + near[1, b].astype(f32)).astype(bf16)
+        far_copy(k).start()
+    for k in order:
+        b = lax.rem(col + k, N)
+        near_copy(0, k).wait_recv()
+        far_copy(k).wait_recv()
+        total = cells_part[row, b].astype(f32) + near[0, b].astype(f32) + far[b].astype(f32)
+        if k == 0:
+            cells_out[...] = total
+        else:
+            outgoing[b] = total.astype(bf16)
+            cells_copy(k).start()
+    total = probe_part[col].astype(f32)
+    for k in range(1, N):
+        probe_copy(k).wait_recv()
+        total += probe_in[k - 1].astype(f32)
+    probe_all[row] = total.astype(bf16)
+    sent = [mode_copy(18, row, across), mode_copy(19, row, sibling)]
+    for copy in sent:
+        copy.start()
+    mode_copy(18, across, across).wait_recv()
+    forwarded = mode_copy(20, across, sibling)
+    forwarded.start()
+    sent.append(forwarded)
+    for k in range(1, N):
+        cells_copy(k).wait_recv()
+        cells_out[...] += cells_in[k - 1].astype(f32)
+    mode_copy(19, sibling, sibling).wait_recv()
+    mode_copy(20, opposite, sibling).wait_recv()
+    probe_out[...] = probe_all[...].astype(f32)
+    for copy in sent:
+        copy.wait_send()
+    for k in range(N):
+        near_copy(0, k).wait_send()
+        near_copy(1, k).wait_send()
+        far_copy(k).wait_send()
+        if k > 0:
+            probe_copy(k).wait_send()
+            cells_copy(k).wait_send()
 
 
 def mul(left, right):
@@ -720,7 +762,7 @@
         cut,
         grid=(POS_AVG,),
         in_specs=[scalars, whole(*cells.shape), ANY],
-        out_specs=[per_slot, ANY],
+        out_specs=[per_slot, whole(N, POS_AVG, *amplitudes.shape[1:])],
         scratch_shapes=[window, pltpu.SemaphoreType.DMA((POS_AVG * N,))],
         out_shape=[
             jax.ShapeDtypeStruct((POS_AVG,) + plane[1:], bf16),
@@ -761,15 +803,26 @@
         compiler_params=pltpu.CompilerParams(vmem_limit_bytes=LIMIT),
         name="place",
     )(meta_all, terms)
-    probe_parts, cells_parts = communicate(
-        scatter_gradients, 4, 8, [(probe_part.shape, bf16), (cells_part.shape, bf16)], probe_part, cells_part
-    )
-    probe_sum = jnp.sum(probe_parts.astype(f32), axis=0).astype(bf16)
-    cells_sum = jnp.sum(cells_parts.astype(f32), axis=0).astype(bf16)
-    cells_last, probe_last = communicate(
-        finish_gradients, 5, 8, [(cells_sum.shape, bf16), ((N,) + probe_sum.shape, bf16)], cells_sum, probe_sum
-    )
-    return jnp.sum(cells_last.astype(f32), axis=0), probe_last.astype(f32)
+    strip = (N,) + object_field.shape
+    object_grad, probe_grad = pl.pallas_call(
+        reduce_gradients,
+        in_specs=[WHOLE, WHOLE],
+        out_specs=[WHOLE, WHOLE],
+        out_shape=[jax.ShapeDtypeStruct(object_field.shape, f32), jax.ShapeDtypeStruct(probe.shape, f32)],
+        scratch_shapes=[
+            pltpu.VMEM((N - 1,) + mode_shape, bf16),
+            pltpu.VMEM((2,) + strip, bf16),
+            pltpu.VMEM(strip, bf16),
+            pltpu.VMEM(strip, bf16),
+            pltpu.VMEM(strip, bf16),
+            pltpu.VMEM((N - 1,) + object_field.shape, bf16),
+            pltpu.VMEM((N,) + mode_shape, bf16),
+            pltpu.SemaphoreType.DMA((2, 21)),
+        ],
+        compiler_params=pltpu.CompilerParams(collective_id=3, has_side_effects=True, vmem_limit_bytes=LIMIT),
+        name="reduce_gradients",
+    )(probe_part, cells_part)
+    return object_grad, probe_grad
 
 
 def solution(mesh):

time: 201 us -> 153 us (0.76)
  Pallas kernels: 188 us -> 145 us
  other arithmetic: 9.27 us -> 0.75 us
  local copies, waits for them, and re-layouts: 0.52 us -> 5.27 us
    pallas_call x1, Pallas kernels: 51.6 us -> 5.99 us  [balanced_device(): pl.pallas_call(cut, grid=(POS_AVG,), in_specs=[scalars, whole(*cells.shap...]
    reduce_sum x3 -> x0, other arithmetic: 5.69 us -> none  [the longest x1 2.94 us: balanced_device(): cells_sum = jnp.sum(cells_parts.astype(f32), axis=0).astype(bf16)]
    unnamed x2, local copies, waits for them, and re-layouts: 0.01 us -> 4.75 us
    convert_element_type x1 -> x0, other arithmetic: 2.83 us -> none  [balanced_device(): return (jnp.sum(cells_last.astype(f32), axis=0), probe_last.astype(f32))]
    pallas_call x2 -> x1, Pallas kernels: 43.1 us -> 45.8 us  [balanced_device(): pl.pallas_call(reduce_gradients, in_specs=[WHOLE, WHOLE], out_specs=[WHOL...]
where the time goes in v4:
time: 153 us; the launch traced here: 152 us
  Pallas kernels  145 us (95%)
  local copies, waits for them, and re-layouts  5.27 us (3%)
    pallas_call x1, Pallas kernels, balanced_device(): pl.pallas_call(propagate, in_specs=[WHOLE, WHOLE, ANY, WHOLE, WHOLE], out...  49.9 us
    pallas_call x1, Pallas kernels, balanced_device(): pl.pallas_call(reduce_gradients, in_specs=[WHOLE, WHOLE], out_specs=[WHOL...  45.8 us
    pallas_call x1, Pallas kernels, balanced_device(): pl.pallas_call(spread_inputs, in_specs=[ANY, WHOLE, ANY, ANY], out_specs=...  36.8 us
    pallas_call x1, Pallas kernels, balanced_device(): pl.pallas_call(place, grid=(POS_AVG,), in_specs=[scalars, per_slot], out_...  6.71 us
    pallas_call x1, Pallas kernels, balanced_device(): pl.pallas_call(cut, grid=(POS_AVG,), in_specs=[scalars, whole(*cells.shap...  5.99 us
    unnamed x2, local copies, waits for them, and re-layouts  4.75 us

profile of v4, /device:TPU:9, one launch (start us, length us, event | category | flops | bytes accessed | tf_op | source)
XLA Modules:
  0.0 152.5 jit_solution(4507693458973210537)
XLA Ops:
  1.3 0.7 pad_add_fusion
  2.0 0.5 pad_bitcast_fusion.meta
  2.5 36.8 %spread_inputs.1 = (s32[4,1,128]{2,1,0:T(1,128)}, bf16[4,2,128,512]{3,2,1,0:T(8,128)(2,1)}, bf16[4,4,2,128,256]{4,3,2,1,0:T(8,128)(2,1)}, bf16[4,6,128,512]{3,2,1,0:T(8,128)(2,1)}) custom-call(s32[1,128]{1,0:T(1,128)} %pad_bitcast_fusion.meta, f32[2,128,256]{2,1,0:T(8,128)} %cells.1, f32[4,2,128,512]{3,2,1,0:T(8,128)} %probe.1, f32[6,128,512]{2,1,0:T(8,128)} %frames.1), custom_call_target="tpu_custom_call" | custom-call | tf_op jit(solution)/shard_map/spread_inputs/pallas_call | solution.py:732
  39.3 6.0 %cut.1 = (bf16[3,2,512,512]{3,2,1,0:T(8,128)(2,1)}, bf16[4,3,128,512]{3,2,1,0:T(8,128)(2,1)}) custom-call(s32[4,1,128]{2,1,0:T(1,128)} %get-tuple-element.10.meta, bf16[4,4,2,128,256]{4,3,2,1,0:T(8,128)(2,1)} %get-tuple-element.11.cells, bf16[4,6,128,512]{3,2,1,0:T(8,128)(2,1)} %get-tuple-element.12.frames_all), custom_call_target="tpu_custom_call" | custom-call | tf_op jit(solution)/shard_map/cut/pallas_call | solution.py:761
  45.3 49.9 %propagate.1 = (bf16[4,2,128,512]{3,2,1,0:T(8,128)(2,1)}, f32[3,2,512,512]{3,2,1,0:T(8,128)}) custom-call(bf16[3,2,512,512]{3,2,1,0:T(8,128)(2,1)} %get-tuple-element.13.patch, bf16[4,2,128,512]{3,2,1,0:T(8,128)(2,1)} %get-tuple-element.14.probe, bf16[4,3,128,512]{3,2,1,0:T(8,128)(2,1)} %get-tuple-element.15.frames, bf16[1024,1024]{1,0:T(8,128)(2,1)} %constant.6.clone.table, ...), custom_call_target="tpu_custom_call" | custom-call | tf_op jit(solution)/shard_map/propagate/pallas_call | solution.py:774
  95.2 6.7 %place.1.cells_part = bf16[4,4,2,128,256]{4,3,2,1,0:T(8,128)(2,1)} custom-call(s32[4,1,128]{2,1,0:T(1,128)} %get-tuple-element.10.meta, f32[3,2,512,512]{3,2,1,0:T(8,128)} %get-tuple-element.17.terms), custom_call_target="tpu_custom_call" | custom-call | tf_op jit(solution)/shard_map/place/pallas_call | solution.py:796
  101.9 45.8 %reduce_gradients.1 = (f32[2,128,256]{2,1,0:T(8,128)}, f32[4,2,128,512]{3,2,1,0:T(8,128)}) custom-call(bf16[4,2,128,512]{3,2,1,0:T(8,128)(2,1)} %get-tuple-element.16.probe_part, bf16[4,4,2,128,256]{4,3,2,1,0:T(8,128)(2,1)} %place.1.cells_part), custom_call_target="tpu_custom_call" | custom-call | tf_op jit(solution)/shard_map/reduce_gradients/pallas_call | solution.py:807
  147.7 1.7 %copy.13 = f32[2,128,256]{2,1,0:T(8,128)} copy(f32[2,128,256]{2,1,0:T(8,128)} %get-tuple-element.20) | data formatting | bytes 524288
  149.4 3.1 %copy.14 = f32[4,2,128,512]{3,2,1,0:T(8,128)} copy(f32[4,2,128,512]{3,2,1,0:T(8,128)} %get-tuple-element.21) | data formatting | bytes 4194304

commit v5 on v4

--- a/solution.py
+++ b/solution.py
@@ -401,9 +401,13 @@
 
 
 def propagate(
-    patch, probe, frames, table, table_t, probe_out, terms, field, power, parts, scale, measured, wide, tall, total, sems
+    patch, probe, frames, table, table_t, probe_out, terms_out,
+    terms, field, power, near, relay, far, scale, measured, wide, tall, total, sems, local
 ):
     row, col = lax.axis_index("rows"), lax.axis_index("cols")
+    sibling = row + 1 - 2 * lax.rem(row, 2)
+    across = lax.rem(row + 2, N)
+    opposite = lax.rem(sibling + 2, N)
     length = patch.shape[-1]
     quarter = length // N
     f32, bf16 = jnp.float32, jnp.bfloat16
@@ -420,24 +424,34 @@
         for k in range(1, N):
             frame_copy(lax.rem(col + k, N)).start()
 
-    def power_copy(p, k):
-        to = lax.rem(row + k, N)
-        return remote(power.at[p, to], parts.at[p, k - 1], sems, p * 3 + k - 1, {"rows": to})
-
-    def scale_copy(p, k, index):
-        to = lax.rem(row + k, N)
-        return remote(scale.at[p, index], scale.at[p, index], sems, 9 + p * 3 + k - 1, {"rows": to})
+    def near_copy(p, half):
+        quarters = opposite if half else sibling
+        return remote(power.at[p, quarters], near.at[p, half], sems, 2 * p + half, {"rows": sibling})
+
+    def far_copy(p):
+        return remote(relay.at[p], far.at[p], sems, 6 + p, {"rows": across})
+
+    def scale_copy(p, kind, index):
+        to = across if kind == 0 else sibling
+        return remote(scale.at[p, index], scale.at[p, index], sems, 9 + 3 * kind + p, {"rows": to})
+
+    def pass_on(p):
+        near_copy(p, 1).wait_recv()
+        relay[p] = (power[p, across].astype(f32) + near[p, 1].astype(f32)).astype(bf16)
+        far_copy(p).start()
 
     def factors(p):
-        for k in range(1, N):
-            power_copy(p, k).wait_recv()
-        intensity = power[p, row].astype(f32)
-        for k in range(1, N):
-            intensity += parts[p, k - 1].astype(f32)
+        near_copy(p, 0).wait_recv()
+        far_copy(p).wait_recv()
+        intensity = power[p, row].astype(f32) + near[p, 0].astype(f32) + far[p].astype(f32)
         amplitude = measured[p].astype(f32).T
         scale[p, row] = (1.0 - amplitude * lax.rsqrt(jnp.maximum(intensity, 0.25))).astype(bf16)
-        for k in range(1, N):
-            scale_copy(p, k, row).start()
+        scale_copy(p, 0, row).start()
+        scale_copy(p, 1, row).start()
+
+    def hand_over(p):
+        scale_copy(p, 0, across).wait_recv()
+        scale_copy(p, 2, across).start()
 
     def transform(p, carry):
         probe_real = probe[:, 0].reshape(length, length).astype(f32)
@@ -454,33 +468,37 @@
         square = result[:length] * result[:length] + result[length:] * result[length:]
         for q in range(N):
             power[p, q] = square[:, q * quarter : (q + 1) * quarter].astype(bf16)
-        for k in range(1, N):
-            power_copy(p, k).start()
-
-        @pl.when(p == 1)
-        def _():
-            @pl.when(row == col)
-            def _():
-                local_frames.wait()
-
-            for k in range(1, N):
-
-                @pl.when(lax.rem(row + k, N) == col)
-                def _():
-                    remote(measured, measured, sems, 18 + k, {"cols": row}).wait_recv()
+        near_copy(p, 1).start()
+        near_copy(p, 0).start()
 
         @pl.when(p >= 1)
         def _():
-            factors(p - 1)
+            pass_on(p - 1)
 
         return carry
 
     lax.fori_loop(0, POS_AVG, transform, 0)
+    pass_on(POS_AVG - 1)
+
+    @pl.when(row == col)
+    def _():
+        local_frames.wait()
+
+    for k in range(1, N):
+
+        @pl.when(lax.rem(row + k, N) == col)
+        def _():
+            remote(measured, measured, sems, 18 + k, {"cols": row}).wait_recv()
+
+    for p in range(POS_AVG):
+        factors(p)
+        if p > 0:
+            hand_over(p - 1)
     total[...] = jnp.zeros(total.shape, f32)
 
     def back_transform(p, carry):
-        for k in range(1, N):
-            scale_copy(p, k, lax.rem(row + N - k, N)).wait_recv()
+        scale_copy(p, 1, sibling).wait_recv()
+        scale_copy(p, 2, opposite).wait_recv()
         for q in range(N):
             lanes = pl.ds(q * quarter, quarter)
             gain = scale[p, q].astype(f32)
@@ -495,6 +513,7 @@
         probe_imag = probe[:, 1].reshape(length, length).astype(f32)
         terms[p, 0] = probe_real * back_real + probe_imag * back_imag
         terms[p, 1] = probe_real * back_imag - probe_imag * back_real
+        pltpu.make_async_copy(terms.at[p], terms_out.at[p], local.at[p]).start()
         patch_real = patch[p, 0].astype(f32)
         patch_imag = patch[p, 1].astype(f32)
         total[0] += patch_real * back_real + patch_imag * back_imag
@@ -502,7 +521,7 @@
 
         @pl.when(p == 0)
         def _():
-            factors(POS_AVG - 1)
+            hand_over(POS_AVG - 1)
 
         return carry
 
@@ -512,9 +531,13 @@
             probe_out[b, part] = total[part, b * quarter : (b + 1) * quarter].astype(bf16)
 
     def finish(p, carry):
-        for k in range(1, N):
-            power_copy(p, k).wait_send()
-            scale_copy(p, k, row).wait_send()
+        near_copy(p, 0).wait_send()
+        near_copy(p, 1).wait_send()
+        far_copy(p).wait_send()
+        scale_copy(p, 0, row).wait_send()
+        scale_copy(p, 1, row).wait_send()
+        scale_copy(p, 2, across).wait_send()
+        pltpu.make_async_copy(terms.at[p], terms_out.at[p], local.at[p]).wait()
         return carry
 
     lax.fori_loop(0, POS_AVG, finish, 0)
@@ -525,8 +548,64 @@
             frame_copy(lax.rem(col + k, N)).wait_send()
 
 
+class LineSum:
+    def __init__(self, blocks, outgoing, from_left, from_right, sems, base):
+        self.blocks, self.outgoing, self.from_left, self.from_right = blocks, outgoing, from_left, from_right
+        self.sems, self.base = sems, base
+        self.col = lax.axis_index("cols")
+
+    def copy(self, d, rightward):
+        col = self.col
+        to = lax.rem(col + 1, N) if rightward else lax.rem(col + N - 1, N)
+        dst = self.from_left if rightward else self.from_right
+        slot = self.base + d + (0 if rightward else N)
+        return remote(self.outgoing.at[d], dst.at[d], self.sems, slot, {"cols": to})
+
+    def step(self, d, rightward):
+        col = self.col
+        landed = self.from_left if rightward else self.from_right
+        first = 0 if rightward else N - 1
+
+        @pl.when((col < d) if rightward else (col > d))
+        def _():
+            @pl.when(col == first)
+            def _():
+                self.outgoing[d] = self.blocks(d).astype(jnp.bfloat16)
+
+            @pl.when(col != first)
+            def _():
+                self.copy(d, rightward).wait_recv()
+                self.outgoing[d] = (self.blocks(d) + landed[d].astype(jnp.float32)).astype(jnp.bfloat16)
+
+            self.copy(d, rightward).start()
+
+    def finish(self, out):
+        col = self.col
+        out[...] = self.blocks(col)
+
+        @pl.when(col > 0)
+        def _():
+            self.copy(col, True).wait_recv()
+            out[...] += self.from_left[col].astype(jnp.float32)
+
+        @pl.when(col < N - 1)
+        def _():
+            self.copy(col, False).wait_recv()
+            out[...] += self.from_right[col].astype(jnp.float32)
+
+    def wait_sent(self):
+        for d in range(N):
+            for rightward in (True, False):
+
+                @pl.when((self.col < d) if rightward else (self.col > d))
+                def _():
+                    self.copy(d, rightward).wait_send()
+
+
 def reduce_gradients(
-    probe_part, cells_part, cells_out, probe_out, probe_in, near, far, relay, outgoing, cells_in, probe_all, sems
+    probe_part, cells_part, cells_out, probe_out,
+    near, far, relay, cells_total, cells_line, cells_left, cells_right,
+    probe_line, probe_left, probe_right, probe_total, probe_all, sems,
 ):
     f32, bf16 = jnp.float32, jnp.bfloat16
     row, col = lax.axis_index("rows"), lax.axis_index("cols")
@@ -534,75 +613,61 @@
     across = lax.rem(row + 2, N)
     opposite = lax.rem(sibling + 2, N)
     greet(("rows", "cols"))
-
-    def probe_copy(k):
-        to = lax.rem(col + k, N)
-        return remote(probe_part.at[to], probe_in.at[k - 1], sems, k - 1, {"cols": to})
-
-    def near_copy(half, k):
-        b = lax.rem(col + k, N)
+    modes = LineSum(lambda d: probe_part[d].astype(f32), probe_line, probe_left, probe_right, sems, 0)
+    cells = LineSum(lambda d: cells_total[d], cells_line, cells_left, cells_right, sems, 8)
+
+    def near_copy(half, b):
         strip = opposite if half else sibling
-        return remote(cells_part.at[strip, b], near.at[half, b], sems, 3 + 4 * half + k, {"rows": sibling})
-
-    def far_copy(k):
-        b = lax.rem(col + k, N)
-        return remote(relay.at[b], far.at[b], sems, 11 + k, {"rows": across})
-
-    def cells_copy(k):
-        b = lax.rem(col + k, N)
-        return remote(outgoing.at[b], cells_in.at[k - 1], sems, 14 + k, {"cols": b})
+        return remote(cells_part.at[strip, b], near.at[half, b], sems, 16 + 4 * half + b, {"rows": sibling})
+
+    def far_copy(b):
+        return remote(relay.at[b], far.at[b], sems, 24 + b, {"rows": across})
 
     def mode_copy(slot, index, to):
         return remote(probe_all.at[index], probe_all.at[index], sems, slot, {"rows": to})
 
-    order = (1, 2, 3, 0)
-    for k in range(1, N):
-        probe_copy(k).start()
+    modes.step(N - 1, True)
+    modes.step(0, False)
     for half in (1, 0):
-        for k in order:
-            near_copy(half, k).start()
-    for k in order:
-        b = lax.rem(col + k, N)
-        near_copy(1, k).wait_recv()
+        for b in range(N):
+            near_copy(half, b).start()
+    for b in range(N):
+        near_copy(1, b).wait_recv()
         relay[b] = (cells_part[across, b].astype(f32) + near[1, b].astype(f32)).astype(bf16)
-        far_copy(k).start()
-    for k in order:
-        b = lax.rem(col + k, N)
-        near_copy(0, k).wait_recv()
-        far_copy(k).wait_recv()
-        total = cells_part[row, b].astype(f32) + near[0, b].astype(f32) + far[b].astype(f32)
-        if k == 0:
-            cells_out[...] = total
-        else:
-            outgoing[b] = total.astype(bf16)
-            cells_copy(k).start()
-    total = probe_part[col].astype(f32)
-    for k in range(1, N):
-        probe_copy(k).wait_recv()
-        total += probe_in[k - 1].astype(f32)
-    probe_all[row] = total.astype(bf16)
-    sent = [mode_copy(18, row, across), mode_copy(19, row, sibling)]
+        far_copy(b).start()
+    for distance in range(1, N - 1):
+        modes.step(N - 1 - distance, True)
+        modes.step(distance, False)
+    for b in range(N):
+        near_copy(0, b).wait_recv()
+        far_copy(b).wait_recv()
+        cells_total[b] = cells_part[row, b].astype(f32) + near[0, b].astype(f32) + far[b].astype(f32)
+    cells.step(N - 1, True)
+    cells.step(0, False)
+    modes.finish(probe_total)
+    probe_all[row] = probe_total[...].astype(bf16)
+    sent = [mode_copy(28, row, across), mode_copy(29, row, sibling)]
     for copy in sent:
         copy.start()
-    mode_copy(18, across, across).wait_recv()
-    forwarded = mode_copy(20, across, sibling)
+    for distance in range(1, N - 1):
+        cells.step(N - 1 - distance, True)
+        cells.step(distance, False)
+    mode_copy(28, across, across).wait_recv()
+    forwarded = mode_copy(30, across, sibling)
     forwarded.start()
     sent.append(forwarded)
-    for k in range(1, N):
-        cells_copy(k).wait_recv()
-        cells_out[...] += cells_in[k - 1].astype(f32)
-    mode_copy(19, sibling, sibling).wait_recv()
-    mode_copy(20, opposite, sibling).wait_recv()
+    mode_copy(29, sibling, sibling).wait_recv()
+    mode_copy(30, opposite, sibling).wait_recv()
     probe_out[...] = probe_all[...].astype(f32)
+    cells.finish(cells_out)
     for copy in sent:
         copy.wait_send()
-    for k in range(N):
-        near_copy(0, k).wait_send()
-        near_copy(1, k).wait_send()
-        far_copy(k).wait_send()
-        if k > 0:
-            probe_copy(k).wait_send()
-            cells_copy(k).wait_send()
+    for b in range(N):
+        near_copy(0, b).wait_send()
+        near_copy(1, b).wait_send()
+        far_copy(b).wait_send()
+    modes.wait_sent()
+    cells.wait_sent()
 
 
 def mul(left, right):
@@ -774,21 +839,25 @@
     probe_part, terms = pl.pallas_call(
         propagate,
         in_specs=[WHOLE, WHOLE, ANY, WHOLE, WHOLE],
-        out_specs=[WHOLE, WHOLE],
+        out_specs=[WHOLE, ANY],
         out_shape=[
             jax.ShapeDtypeStruct(mode_all.shape, bf16),
             jax.ShapeDtypeStruct((POS_AVG,) + plane[1:], f32),
         ],
         scratch_shapes=[
+            pltpu.VMEM((POS_AVG,) + plane[1:], f32),
             pltpu.VMEM((POS_AVG, 2 * length, length), f32),
             pltpu.VMEM(quarters, bf16),
-            pltpu.VMEM((POS_AVG, N - 1) + quarters[2:], bf16),
+            pltpu.VMEM((POS_AVG, 2) + quarters[2:], bf16),
+            pltpu.VMEM((POS_AVG,) + quarters[2:], bf16),
+            pltpu.VMEM((POS_AVG,) + quarters[2:], bf16),
             pltpu.VMEM(quarters, bf16),
             pltpu.VMEM(frames.shape[1:], bf16),
             pltpu.VMEM((length, 2 * length), bf16),
             pltpu.VMEM((2 * length, length), bf16),
             pltpu.VMEM((2, length, length), f32),
             pltpu.SemaphoreType.DMA((2, 22)),
+            pltpu.SemaphoreType.DMA((POS_AVG,)),
         ],
         compiler_params=pltpu.CompilerParams(collective_id=2, has_side_effects=True, vmem_limit_bytes=LIMIT),
         name="propagate",
@@ -810,14 +879,19 @@
         out_specs=[WHOLE, WHOLE],
         out_shape=[jax.ShapeDtypeStruct(object_field.shape, f32), jax.ShapeDtypeStruct(probe.shape, f32)],
         scratch_shapes=[
-            pltpu.VMEM((N - 1,) + mode_shape, bf16),
             pltpu.VMEM((2,) + strip, bf16),
             pltpu.VMEM(strip, bf16),
             pltpu.VMEM(strip, bf16),
+            pltpu.VMEM(strip, f32),
             pltpu.VMEM(strip, bf16),
-            pltpu.VMEM((N - 1,) + object_field.shape, bf16),
+            pltpu.VMEM(strip, bf16),
+            pltpu.VMEM(strip, bf16),
             pltpu.VMEM((N,) + mode_shape, bf16),
-            pltpu.SemaphoreType.DMA((2, 21)),
+            pltpu.VMEM((N,) + mode_shape, bf16),
+            pltpu.VMEM((N,) + mode_shape, bf16),
+            pltpu.VMEM(mode_shape, f32),
+            pltpu.VMEM((N,) + mode_shape, bf16),
+            pltpu.SemaphoreType.DMA((2, 31)),
         ],
         compiler_params=pltpu.CompilerParams(collective_id=3, has_side_effects=True, vmem_limit_bytes=LIMIT),
         name="reduce_gradients",

time: 153 us -> 159 us (1.039)
  Pallas kernels: 145 us -> 151 us
    pallas_call x1, Pallas kernels: 45.8 us -> 60.4 us  [balanced_device(): pl.pallas_call(reduce_gradients, in_specs=[WHOLE, WHOLE], out_specs=[WHOL...]
    pallas_call x1, Pallas kernels: 49.9 us -> 40.9 us  [balanced_device(): pl.pallas_call(propagate, in_specs=[WHOLE, WHOLE, ANY, WHOLE, WHOLE], out...]
where the time goes in v5:
time: 159 us; the launch traced here: 158 us
  Pallas kernels  151 us (95%)
  local copies, waits for them, and re-layouts  5.27 us (3%)
    pallas_call x1, Pallas kernels, balanced_device(): pl.pallas_call(reduce_gradients, in_specs=[WHOLE, WHOLE], out_specs=[WHOL...  60.4 us
    pallas_call x1, Pallas kernels, balanced_device(): pl.pallas_call(propagate, in_specs=[WHOLE, WHOLE, ANY, WHOLE, WHOLE], out...  40.9 us
    pallas_call x1, Pallas kernels, balanced_device(): pl.pallas_call(spread_inputs, in_specs=[ANY, WHOLE, ANY, ANY], out_specs=...  36.8 us
    pallas_call x1, Pallas kernels, balanced_device(): pl.pallas_call(place, grid=(POS_AVG,), in_specs=[scalars, per_slot], out_...  6.8 us
    pallas_call x1, Pallas kernels, balanced_device(): pl.pallas_call(cut, grid=(POS_AVG,), in_specs=[scalars, whole(*cells.shap...  5.99 us
    unnamed x2, local copies, waits for them, and re-layouts  4.75 us

profile of v5, /device:TPU:9, one launch (start us, length us, event | category | flops | bytes accessed | tf_op | source)
XLA Modules:
  0.0 158.2 jit_solution(3926293895134388820)
XLA Ops:
  1.3 0.7 pad_add_fusion
  2.0 0.5 pad_bitcast_fusion.meta
  2.5 36.8 %spread_inputs.1 = (s32[4,1,128]{2,1,0:T(1,128)}, bf16[4,2,128,512]{3,2,1,0:T(8,128)(2,1)}, bf16[4,4,2,128,256]{4,3,2,1,0:T(8,128)(2,1)}, bf16[4,6,128,512]{3,2,1,0:T(8,128)(2,1)}) custom-call(s32[1,128]{1,0:T(1,128)} %pad_bitcast_fusion.meta, f32[2,128,256]{2,1,0:T(8,128)} %cells.1, f32[4,2,128,512]{3,2,1,0:T(8,128)} %probe.1, f32[6,128,512]{2,1,0:T(8,128)} %frames.1), custom_call_target="tpu_custom_call" | custom-call | tf_op jit(solution)/shard_map/spread_inputs/pallas_call | solution.py:797
  39.3 6.0 %cut.1 = (bf16[3,2,512,512]{3,2,1,0:T(8,128)(2,1)}, bf16[4,3,128,512]{3,2,1,0:T(8,128)(2,1)}) custom-call(s32[4,1,128]{2,1,0:T(1,128)} %get-tuple-element.10.meta, bf16[4,4,2,128,256]{4,3,2,1,0:T(8,128)(2,1)} %get-tuple-element.11.cells, bf16[4,6,128,512]{3,2,1,0:T(8,128)(2,1)} %get-tuple-element.12.frames_all), custom_call_target="tpu_custom_call" | custom-call | tf_op jit(solution)/shard_map/cut/pallas_call | solution.py:826
  45.3 40.9 %propagate.1 = (bf16[4,2,128,512]{3,2,1,0:T(8,128)(2,1)}, f32[3,2,512,512]{3,2,1,0:T(8,128)}) custom-call(bf16[3,2,512,512]{3,2,1,0:T(8,128)(2,1)} %get-tuple-element.13.patch, bf16[4,2,128,512]{3,2,1,0:T(8,128)(2,1)} %get-tuple-element.14.probe, bf16[4,3,128,512]{3,2,1,0:T(8,128)(2,1)} %get-tuple-element.15.frames, bf16[1024,1024]{1,0:T(8,128)(2,1)} %constant.6.clone.table, ...), custom_call_target="tpu_custom_call" | custom-call | tf_op jit(solution)/shard_map/propagate/pallas_call | solution.py:839
  86.2 6.8 %place.1.cells_part = bf16[4,4,2,128,256]{4,3,2,1,0:T(8,128)(2,1)} custom-call(s32[4,1,128]{2,1,0:T(1,128)} %get-tuple-element.10.meta, f32[3,2,512,512]{3,2,1,0:T(8,128)} %get-tuple-element.17.terms), custom_call_target="tpu_custom_call" | custom-call | tf_op jit(solution)/shard_map/place/pallas_call | solution.py:865
  93.0 60.4 %reduce_gradients.1 = (f32[2,128,256]{2,1,0:T(8,128)}, f32[4,2,128,512]{3,2,1,0:T(8,128)}) custom-call(bf16[4,2,128,512]{3,2,1,0:T(8,128)(2,1)} %get-tuple-element.16.probe_part, bf16[4,4,2,128,256]{4,3,2,1,0:T(8,128)(2,1)} %place.1.cells_part), custom_call_target="tpu_custom_call" | custom-call | tf_op jit(solution)/shard_map/reduce_gradients/pallas_call | solution.py:876
  153.4 1.7 %copy.13 = f32[2,128,256]{2,1,0:T(8,128)} copy(f32[2,128,256]{2,1,0:T(8,128)} %get-tuple-element.20) | data formatting | bytes 524288
  155.1 3.1 %copy.14 = f32[4,2,128,512]{3,2,1,0:T(8,128)} copy(f32[4,2,128,512]{3,2,1,0:T(8,128)} %get-tuple-element.21) | data formatting | bytes 4194304

commit v6 on v4

--- a/solution.py
+++ b/solution.py
@@ -401,9 +401,13 @@
 
 
 def propagate(
-    patch, probe, frames, table, table_t, probe_out, terms, field, power, parts, scale, measured, wide, tall, total, sems
+    patch, probe, frames, table, table_t, probe_out, terms_out,
+    terms, field, power, near, relay, far, scale, measured, wide, tall, total, sems, local
 ):
     row, col = lax.axis_index("rows"), lax.axis_index("cols")
+    sibling = row + 1 - 2 * lax.rem(row, 2)
+    across = lax.rem(row + 2, N)
+    opposite = lax.rem(sibling + 2, N)
     length = patch.shape[-1]
     quarter = length // N
     f32, bf16 = jnp.float32, jnp.bfloat16
@@ -420,24 +424,34 @@
         for k in range(1, N):
             frame_copy(lax.rem(col + k, N)).start()
 
-    def power_copy(p, k):
-        to = lax.rem(row + k, N)
-        return remote(power.at[p, to], parts.at[p, k - 1], sems, p * 3 + k - 1, {"rows": to})
-
-    def scale_copy(p, k, index):
-        to = lax.rem(row + k, N)
-        return remote(scale.at[p, index], scale.at[p, index], sems, 9 + p * 3 + k - 1, {"rows": to})
+    def near_copy(p, half):
+        quarters = opposite if half else sibling
+        return remote(power.at[p, quarters], near.at[p, half], sems, 2 * p + half, {"rows": sibling})
+
+    def far_copy(p):
+        return remote(relay.at[p], far.at[p], sems, 6 + p, {"rows": across})
+
+    def scale_copy(p, kind, index):
+        to = across if kind == 0 else sibling
+        return remote(scale.at[p, index], scale.at[p, index], sems, 9 + 3 * kind + p, {"rows": to})
+
+    def pass_on(p):
+        near_copy(p, 1).wait_recv()
+        relay[p] = (power[p, across].astype(f32) + near[p, 1].astype(f32)).astype(bf16)
+        far_copy(p).start()
 
     def factors(p):
-        for k in range(1, N):
-            power_copy(p, k).wait_recv()
-        intensity = power[p, row].astype(f32)
-        for k in range(1, N):
-            intensity += parts[p, k - 1].astype(f32)
+        near_copy(p, 0).wait_recv()
+        far_copy(p).wait_recv()
+        intensity = power[p, row].astype(f32) + near[p, 0].astype(f32) + far[p].astype(f32)
         amplitude = measured[p].astype(f32).T
         scale[p, row] = (1.0 - amplitude * lax.rsqrt(jnp.maximum(intensity, 0.25))).astype(bf16)
-        for k in range(1, N):
-            scale_copy(p, k, row).start()
+        scale_copy(p, 0, row).start()
+        scale_copy(p, 1, row).start()
+
+    def hand_over(p):
+        scale_copy(p, 0, across).wait_recv()
+        scale_copy(p, 2, across).start()
 
     def transform(p, carry):
         probe_real = probe[:, 0].reshape(length, length).astype(f32)
@@ -454,33 +468,37 @@
         square = result[:length] * result[:length] + result[length:] * result[length:]
         for q in range(N):
             power[p, q] = square[:, q * quarter : (q + 1) * quarter].astype(bf16)
-        for k in range(1, N):
-            power_copy(p, k).start()
-
-        @pl.when(p == 1)
-        def _():
-            @pl.when(row == col)
-            def _():
-                local_frames.wait()
-
-            for k in range(1, N):
-
-                @pl.when(lax.rem(row + k, N) == col)
-                def _():
-                    remote(measured, measured, sems, 18 + k, {"cols": row}).wait_recv()
+        near_copy(p, 1).start()
+        near_copy(p, 0).start()
 
         @pl.when(p >= 1)
         def _():
-            factors(p - 1)
+            pass_on(p - 1)
 
         return carry
 
     lax.fori_loop(0, POS_AVG, transform, 0)
+    pass_on(POS_AVG - 1)
+
+    @pl.when(row == col)
+    def _():
+        local_frames.wait()
+
+    for k in range(1, N):
+
+        @pl.when(lax.rem(row + k, N) == col)
+        def _():
+            remote(measured, measured, sems, 18 + k, {"cols": row}).wait_recv()
+
+    for p in range(POS_AVG):
+        factors(p)
+        if p > 0:
+            hand_over(p - 1)
     total[...] = jnp.zeros(total.shape, f32)
 
     def back_transform(p, carry):
-        for k in range(1, N):
-            scale_copy(p, k, lax.rem(row + N - k, N)).wait_recv()
+        scale_copy(p, 1, sibling).wait_recv()
+        scale_copy(p, 2, opposite).wait_recv()
         for q in range(N):
             lanes = pl.ds(q * quarter, quarter)
             gain = scale[p, q].astype(f32)
@@ -495,6 +513,7 @@
         probe_imag = probe[:, 1].reshape(length, length).astype(f32)
         terms[p, 0] = probe_real * back_real + probe_imag * back_imag
         terms[p, 1] = probe_real * back_imag - probe_imag * back_real
+        pltpu.make_async_copy(terms.at[p], terms_out.at[p], local.at[p]).start()
         patch_real = patch[p, 0].astype(f32)
         patch_imag = patch[p, 1].astype(f32)
         total[0] += patch_real * back_real + patch_imag * back_imag
@@ -502,7 +521,7 @@
 
         @pl.when(p == 0)
         def _():
-            factors(POS_AVG - 1)
+            hand_over(POS_AVG - 1)
 
         return carry
 
@@ -512,9 +531,13 @@
             probe_out[b, part] = total[part, b * quarter : (b + 1) * quarter].astype(bf16)
 
     def finish(p, carry):
-        for k in range(1, N):
-            power_copy(p, k).wait_send()
-            scale_copy(p, k, row).wait_send()
+        near_copy(p, 0).wait_send()
+        near_copy(p, 1).wait_send()
+        far_copy(p).wait_send()
+        scale_copy(p, 0, row).wait_send()
+        scale_copy(p, 1, row).wait_send()
+        scale_copy(p, 2, across).wait_send()
+        pltpu.make_async_copy(terms.at[p], terms_out.at[p], local.at[p]).wait()
         return carry
 
     lax.fori_loop(0, POS_AVG, finish, 0)
@@ -774,21 +797,25 @@
     probe_part, terms = pl.pallas_call(
         propagate,
         in_specs=[WHOLE, WHOLE, ANY, WHOLE, WHOLE],
-        out_specs=[WHOLE, WHOLE],
+        out_specs=[WHOLE, ANY],
         out_shape=[
             jax.ShapeDtypeStruct(mode_all.shape, bf16),
             jax.ShapeDtypeStruct((POS_AVG,) + plane[1:], f32),
         ],
         scratch_shapes=[
+            pltpu.VMEM((POS_AVG,) + plane[1:], f32),
             pltpu.VMEM((POS_AVG, 2 * length, length), f32),
             pltpu.VMEM(quarters, bf16),
-            pltpu.VMEM((POS_AVG, N - 1) + quarters[2:], bf16),
+            pltpu.VMEM((POS_AVG, 2) + quarters[2:], bf16),
+            pltpu.VMEM((POS_AVG,) + quarters[2:], bf16),
+            pltpu.VMEM((POS_AVG,) + quarters[2:], bf16),
             pltpu.VMEM(quarters, bf16),
             pltpu.VMEM(frames.shape[1:], bf16),
             pltpu.VMEM((length, 2 * length), bf16),
             pltpu.VMEM((2 * length, length), bf16),
             pltpu.VMEM((2, length, length), f32),
             pltpu.SemaphoreType.DMA((2, 22)),
+            pltpu.SemaphoreType.DMA((POS_AVG,)),
         ],
         compiler_params=pltpu.CompilerParams(collective_id=2, has_side_effects=True, vmem_limit_bytes=LIMIT),
         name="propagate",

time: 153 us -> 143 us (0.935)
  Pallas kernels: 145 us -> 135 us
    pallas_call x1, Pallas kernels: 49.9 us -> 40.9 us  [balanced_device(): pl.pallas_call(propagate, in_specs=[WHOLE, WHOLE, ANY, WHOLE, WHOLE], out...]
where the time goes in v6:
time: 143 us
  Pallas kernels  135 us (94%)
  local copies, waits for them, and re-layouts  5.27 us (4%)
    pallas_call x1, Pallas kernels, balanced_device(): pl.pallas_call(reduce_gradients, in_specs=[WHOLE, WHOLE], out_specs=[WHOL...  44.9 us
    pallas_call x1, Pallas kernels, balanced_device(): pl.pallas_call(propagate, in_specs=[WHOLE, WHOLE, ANY, WHOLE, WHOLE], out...  40.9 us
    pallas_call x1, Pallas kernels, balanced_device(): pl.pallas_call(spread_inputs, in_specs=[ANY, WHOLE, ANY, ANY], out_specs=...  36.8 us
    pallas_call x1, Pallas kernels, balanced_device(): pl.pallas_call(place, grid=(POS_AVG,), in_specs=[scalars, per_slot], out_...  6.81 us
    pallas_call x1, Pallas kernels, balanced_device(): pl.pallas_call(cut, grid=(POS_AVG,), in_specs=[scalars, whole(*cells.shap...  5.99 us
    unnamed x2, local copies, waits for them, and re-layouts  4.75 us

profile of v6, /device:TPU:9, one launch (start us, length us, event | category | flops | bytes accessed | tf_op | source)
XLA Modules:
  0.0 142.7 jit_solution(9318440363734586733)
XLA Ops:
  1.3 0.7 pad_add_fusion
  2.0 0.5 pad_bitcast_fusion.meta
  2.5 36.8 %spread_inputs.1 = (s32[4,1,128]{2,1,0:T(1,128)}, bf16[4,2,128,512]{3,2,1,0:T(8,128)(2,1)}, bf16[4,4,2,128,256]{4,3,2,1,0:T(8,128)(2,1)}, bf16[4,6,128,512]{3,2,1,0:T(8,128)(2,1)}) custom-call(s32[1,128]{1,0:T(1,128)} %pad_bitcast_fusion.meta, f32[2,128,256]{2,1,0:T(8,128)} %cells.1, f32[4,2,128,512]{3,2,1,0:T(8,128)} %probe.1, f32[6,128,512]{2,1,0:T(8,128)} %frames.1), custom_call_target="tpu_custom_call" | custom-call | tf_op jit(solution)/shard_map/spread_inputs/pallas_call | solution.py:755
  39.3 6.0 %cut.1 = (bf16[3,2,512,512]{3,2,1,0:T(8,128)(2,1)}, bf16[4,3,128,512]{3,2,1,0:T(8,128)(2,1)}) custom-call(s32[4,1,128]{2,1,0:T(1,128)} %get-tuple-element.10.meta, bf16[4,4,2,128,256]{4,3,2,1,0:T(8,128)(2,1)} %get-tuple-element.11.cells, bf16[4,6,128,512]{3,2,1,0:T(8,128)(2,1)} %get-tuple-element.12.frames_all), custom_call_target="tpu_custom_call" | custom-call | tf_op jit(solution)/shard_map/cut/pallas_call | solution.py:784
  45.3 40.9 %propagate.1 = (bf16[4,2,128,512]{3,2,1,0:T(8,128)(2,1)}, f32[3,2,512,512]{3,2,1,0:T(8,128)}) custom-call(bf16[3,2,512,512]{3,2,1,0:T(8,128)(2,1)} %get-tuple-element.13.patch, bf16[4,2,128,512]{3,2,1,0:T(8,128)(2,1)} %get-tuple-element.14.probe, bf16[4,3,128,512]{3,2,1,0:T(8,128)(2,1)} %get-tuple-element.15.frames, bf16[1024,1024]{1,0:T(8,128)(2,1)} %constant.6.clone.table, ...), custom_call_target="tpu_custom_call" | custom-call | tf_op jit(solution)/shard_map/propagate/pallas_call | solution.py:797
  86.2 6.8 %place.1.cells_part = bf16[4,4,2,128,256]{4,3,2,1,0:T(8,128)(2,1)} custom-call(s32[4,1,128]{2,1,0:T(1,128)} %get-tuple-element.10.meta, f32[3,2,512,512]{3,2,1,0:T(8,128)} %get-tuple-element.17.terms), custom_call_target="tpu_custom_call" | custom-call | tf_op jit(solution)/shard_map/place/pallas_call | solution.py:823
  93.0 44.9 %reduce_gradients.1 = (f32[2,128,256]{2,1,0:T(8,128)}, f32[4,2,128,512]{3,2,1,0:T(8,128)}) custom-call(bf16[4,2,128,512]{3,2,1,0:T(8,128)(2,1)} %get-tuple-element.16.probe_part, bf16[4,4,2,128,256]{4,3,2,1,0:T(8,128)(2,1)} %place.1.cells_part), custom_call_target="tpu_custom_call" | custom-call | tf_op jit(solution)/shard_map/reduce_gradients/pallas_call | solution.py:834
  137.9 1.7 %copy.13 = f32[2,128,256]{2,1,0:T(8,128)} copy(f32[2,128,256]{2,1,0:T(8,128)} %get-tuple-element.20) | data formatting | bytes 524288
  139.6 3.1 %copy.14 = f32[4,2,128,512]{3,2,1,0:T(8,128)} copy(f32[4,2,128,512]{3,2,1,0:T(8,128)} %get-tuple-element.21) | data formatting | bytes 4194304

commit v7 on v6

--- a/solution.py
+++ b/solution.py
@@ -401,8 +401,8 @@
 
 
 def propagate(
-    patch, probe, frames, table, table_t, probe_out, terms_out,
-    terms, field, power, near, relay, far, scale, measured, wide, tall, total, sems, local
+    patch_in, probe_in, frames, table_in, table_t_in, probe_out, terms_out,
+    patch, probe, table, table_t, terms, field, power, near, relay, far, scale, measured, wide, tall, total, sems, local
 ):
     row, col = lax.axis_index("rows"), lax.axis_index("cols")
     sibling = row + 1 - 2 * lax.rem(row, 2)
@@ -411,6 +411,13 @@
     length = patch.shape[-1]
     quarter = length // N
     f32, bf16 = jnp.float32, jnp.bfloat16
+    sources = (probe_in, patch_in, table_in, table_t_in)
+    loads = [
+        pltpu.make_async_copy(src, dst, local.at[POS_AVG + i])
+        for i, (src, dst) in enumerate(zip(sources, (probe, patch, table, table_t)))
+    ]
+    for load in loads:
+        load.start()
     greet(("rows", "cols"))
 
     def frame_copy(to):
@@ -477,6 +484,8 @@
 
         return carry
 
+    for load in loads:
+        load.wait()
     lax.fori_loop(0, POS_AVG, transform, 0)
     pass_on(POS_AVG - 1)
 
@@ -549,7 +558,7 @@
 
 
 def reduce_gradients(
-    probe_part, cells_part, cells_out, probe_out, probe_in, near, far, relay, outgoing, cells_in, probe_all, sems
+    probe_part, cells_part, cells_out, probe_all, probe_in, near, far, relay, outgoing, cells_in, sems
 ):
     f32, bf16 = jnp.float32, jnp.bfloat16
     row, col = lax.axis_index("rows"), lax.axis_index("cols")
@@ -616,7 +625,6 @@
         cells_out[...] += cells_in[k - 1].astype(f32)
     mode_copy(19, sibling, sibling).wait_recv()
     mode_copy(20, opposite, sibling).wait_recv()
-    probe_out[...] = probe_all[...].astype(f32)
     for copy in sent:
         copy.wait_send()
     for k in range(N):
@@ -796,13 +804,17 @@
     )(meta_all, cells, frames_all)
     probe_part, terms = pl.pallas_call(
         propagate,
-        in_specs=[WHOLE, WHOLE, ANY, WHOLE, WHOLE],
+        in_specs=[ANY] * 5,
         out_specs=[WHOLE, ANY],
         out_shape=[
             jax.ShapeDtypeStruct(mode_all.shape, bf16),
             jax.ShapeDtypeStruct((POS_AVG,) + plane[1:], f32),
         ],
         scratch_shapes=[
+            pltpu.VMEM(patch.shape, bf16),
+            pltpu.VMEM(mode_all.shape, bf16),
+            pltpu.VMEM(table.shape, bf16),
+            pltpu.VMEM(table.shape, bf16),
             pltpu.VMEM((POS_AVG,) + plane[1:], f32),
             pltpu.VMEM((POS_AVG, 2 * length, length), f32),
             pltpu.VMEM(quarters, bf16),
@@ -815,7 +827,7 @@
             pltpu.VMEM((2 * length, length), bf16),
             pltpu.VMEM((2, length, length), f32),
             pltpu.SemaphoreType.DMA((2, 22)),
-            pltpu.SemaphoreType.DMA((POS_AVG,)),
+            pltpu.SemaphoreType.DMA((POS_AVG + 4,)),
         ],
         compiler_params=pltpu.CompilerParams(collective_id=2, has_side_effects=True, vmem_limit_bytes=LIMIT),
         name="propagate",
@@ -835,7 +847,7 @@
         reduce_gradients,
         in_specs=[WHOLE, WHOLE],
         out_specs=[WHOLE, WHOLE],
-        out_shape=[jax.ShapeDtypeStruct(object_field.shape, f32), jax.ShapeDtypeStruct(probe.shape, f32)],
+        out_shape=[jax.ShapeDtypeStruct(object_field.shape, f32), jax.ShapeDtypeStruct(probe.shape, bf16)],
         scratch_shapes=[
             pltpu.VMEM((N - 1,) + mode_shape, bf16),
             pltpu.VMEM((2,) + strip, bf16),
@@ -843,13 +855,12 @@
             pltpu.VMEM(strip, bf16),
             pltpu.VMEM(strip, bf16),
             pltpu.VMEM((N - 1,) + object_field.shape, bf16),
-            pltpu.VMEM((N,) + mode_shape, bf16),
             pltpu.SemaphoreType.DMA((2, 21)),
         ],
         compiler_params=pltpu.CompilerParams(collective_id=3, has_side_effects=True, vmem_limit_bytes=LIMIT),
         name="reduce_gradients",
     )(probe_part, cells_part)
-    return object_grad, probe_grad
+    return object_grad, probe_grad.astype(f32)
 
 
 def solution(mesh):

time: 143 us -> 138 us (0.965)
  local copies, waits for them, and re-layouts: 5.27 us -> 1.22 us
  Pallas kernels: 135 us -> 131 us
  other arithmetic: 0.75 us -> 3.62 us
    unnamed x2 -> x3, local copies, waits for them, and re-layouts: 4.75 us -> 0.71 us
    convert_element_type x0 -> x1, other arithmetic: none -> 2.87 us  [balanced_device(): return (object_grad, probe_grad.astype(f32))]
    pallas_call x1, Pallas kernels: 40.9 us -> 38.2 us  [balanced_device(): pl.pallas_call(propagate, in_specs=[ANY] * 5, out_specs=[WHOLE, ANY], out...]
    pallas_call x1, Pallas kernels: 44.9 us -> 43.3 us  [balanced_device(): pl.pallas_call(reduce_gradients, in_specs=[WHOLE, WHOLE], out_specs=[WHOL...]
where the time goes in v7:
time: 138 us; the launch traced here: 137 us
  Pallas kernels  131 us (95%)
  other arithmetic  3.62 us (3%)
    pallas_call x1, Pallas kernels, balanced_device(): pl.pallas_call(reduce_gradients, in_specs=[WHOLE, WHOLE], out_specs=[WHOL...  43.3 us
    pallas_call x1, Pallas kernels, balanced_device(): pl.pallas_call(propagate, in_specs=[ANY] * 5, out_specs=[WHOLE, ANY], out...  38.2 us
    pallas_call x1, Pallas kernels, balanced_device(): pl.pallas_call(spread_inputs, in_specs=[ANY, WHOLE, ANY, ANY], out_specs=...  36.8 us
    pallas_call x1, Pallas kernels, balanced_device(): pl.pallas_call(place, grid=(POS_AVG,), in_specs=[scalars, per_slot], out_...  6.81 us
    pallas_call x1, Pallas kernels, balanced_device(): pl.pallas_call(cut, grid=(POS_AVG,), in_specs=[scalars, whole(*cells.shap...  5.99 us
    convert_element_type x1, other arithmetic, balanced_device(): return (object_grad, probe_grad.astype(f32))  2.87 us

profile of v7, /device:TPU:9, one launch (start us, length us, event | category | flops | bytes accessed | tf_op | source)
XLA Modules:
  0.0 137.3 jit_solution(17760369502519699871)
XLA Ops:
  1.3 0.7 pad_add_fusion
  2.0 0.5 pad_bitcast_fusion.meta
  2.5 36.8 %spread_inputs.1 = (s32[4,1,128]{2,1,0:T(1,128)}, bf16[4,2,128,512]{3,2,1,0:T(8,128)(2,1)}, bf16[4,4,2,128,256]{4,3,2,1,0:T(8,128)(2,1)}, bf16[4,6,128,512]{3,2,1,0:T(8,128)(2,1)}) custom-call(s32[1,128]{1,0:T(1,128)} %pad_bitcast_fusion.meta, f32[2,128,256]{2,1,0:T(8,128)} %cells.1, f32[4,2,128,512]{3,2,1,0:T(8,128)} %probe.1, f32[6,128,512]{2,1,0:T(8,128)} %frames.1), custom_call_target="tpu_custom_call" | custom-call | tf_op jit(solution)/shard_map/spread_inputs/pallas_call | solution.py:763
  39.3 6.0 %cut.1 = (bf16[3,2,512,512]{3,2,1,0:T(8,128)(2,1)}, bf16[4,3,128,512]{3,2,1,0:T(8,128)(2,1)}) custom-call(s32[4,1,128]{2,1,0:T(1,128)} %get-tuple-element.12.meta, bf16[4,4,2,128,256]{4,3,2,1,0:T(8,128)(2,1)} %get-tuple-element.13.cells, bf16[4,6,128,512]{3,2,1,0:T(8,128)(2,1)} %get-tuple-element.14.frames_all), custom_call_target="tpu_custom_call" | custom-call | tf_op jit(solution)/shard_map/cut/pallas_call | solution.py:792
  45.3 38.2 %propagate.1 = (bf16[4,2,128,512]{3,2,1,0:T(8,128)(2,1)}, f32[3,2,512,512]{3,2,1,0:T(8,128)}) custom-call(bf16[3,2,512,512]{3,2,1,0:T(8,128)(2,1)} %get-tuple-element.15.patch_in, bf16[4,2,128,512]{3,2,1,0:T(8,128)(2,1)} %get-tuple-element.16.probe_in, bf16[4,3,128,512]{3,2,1,0:T(8,128)(2,1)} %get-tuple-element.17.frames, ...), custom_call_target="tpu_custom_call" | custom-call | tf_op jit(solution)/shard_map/propagate/pallas_call | solution.py:805
  83.6 6.8 %place.1.cells_part = bf16[4,4,2,128,256]{4,3,2,1,0:T(8,128)(2,1)} custom-call(s32[4,1,128]{2,1,0:T(1,128)} %get-tuple-element.12.meta, f32[3,2,512,512]{3,2,1,0:T(8,128)} %get-tuple-element.19.terms), custom_call_target="tpu_custom_call" | custom-call | tf_op jit(solution)/shard_map/place/pallas_call | solution.py:835
  90.4 43.3 %reduce_gradients.1 = (f32[2,128,256]{2,1,0:T(8,128)}, bf16[4,2,128,512]{3,2,1,0:T(8,128)(2,1)}) custom-call(bf16[4,2,128,512]{3,2,1,0:T(8,128)(2,1)} %get-tuple-element.18.probe_part, bf16[4,4,2,128,256]{4,3,2,1,0:T(8,128)(2,1)} %place.1.cells_part), custom_call_target="tpu_custom_call" | custom-call | tf_op jit(solution)/shard_map/reduce_gradients/pallas_call | solution.py:846
  133.7 0.0 copy-start
  133.7 2.9 %convert_element_type.3 = f32[4,2,128,512]{3,2,1,0:T(8,128)} convert(bf16[4,2,128,512]{3,2,1,0:T(8,128)(2,1)} %get-tuple-element.21) | non-fusion elementwise | flops 524288 | bytes 3145728 | tf_op jit(solution)/shard_map/convert_element_type | solution.py:863
  136.6 0.0 copy-done
  136.6 0.7 copy.12
Async XLA Ops:
  133.7 2.9 %copy-start = (f32[2,128,256]{2,1,0:T(8,128)S(1)}, f32[2,128,256]{2,1,0:T(8,128)}, u32[]{:S(2)}) copy-start(f32[2,128,256]{2,1,0:T(8,128)} %get-tuple-element.24) | copy-start | bytes 786436
